TPU v7x, 32 devices: a whole 2x2x4 slice. The times are simulated.
32 devices in a mesh: tm: 4 (over z), dof: 8 (over y, x, core).
Axes of the slice: x: 2, y: 2, z: 4, core: 2. Of those that a mesh axis runs over, the one named last changes fastest.
Arguments:
- loads: bfloat16 [1536, 4096], P('tm', 'dof'), may hold values from -6 to 6
- phi: bfloat16 [6144, 4096], P('dof'), may hold values from -0.125 to 0.125
- load_index: int32 [4096], P('dof'), may hold values from 0 to 6143, as said below
- damping: float32 [4096], P('dof'), may hold values from 0.00013020834 to 0.05
- frequency: float32 [4096], P('dof'), may hold values from 0.05 to 1.5
- gains: float32 [1536], P('tm'), may hold values from 0.25 to 1
- shapes: bfloat16 [4096, 16384], P(None, 'dof'), may hold values from -0.09375 to 0.09375
Outputs:
- field: bfloat16 [1536, 16384], P('tm', 'dof')
- history: float32 [4096, 1536], P('dof', 'tm')
Inputs may be any that keep to these rules, and one draw needn't show every extreme that they name: `load_index`: entries k * 512 to (k + 1) * 512 - 1 name rows k * 768 to (k + 1) * 768 - 1; rows may repeat.
All inputs are finite; a program needn't handle non-finite values.
Results may differ from a plain program's by a relative error of at most 0.0049.
Values may be sent and summed in bfloat16 or wider, within the bound.
A program may use at most 128 MiB of HBM per device.

v0:
```python
import jax
import jax.numpy as jnp
from jax import lax
from jax.sharding import PartitionSpec as P


def carried_in(value, axis, join, neutral):
    count, mine = (lax.axis_size(axis), lax.axis_index(axis))
    pieces = jax.tree.map(lambda part: lax.all_gather(part, axis), value)
    subtotal = jax.tree.map(
        lambda part, zero: jnp.full_like(part, 0) + jnp.asarray(zero, part.dtype), value, neutral
    )

    def step(position, subtotal):
        longer = join(subtotal, jax.tree.map(lambda part: part[position], pieces))
        return jax.tree.map(lambda new, old: jnp.where(position < mine, new, old), longer, subtotal)

    return lax.fori_loop(0, count - 1, step, subtotal)


def combine(earlier, later):
    ear, eai, ebr, ebi = earlier
    lar, lai, lbr, lbi = later
    return (
        lar * ear - lai * eai,
        lar * eai + lai * ear,
        lar * ebr - lai * ebi + lbr,
        lar * ebi + lai * ebr + lbi,
    )


def body(loads, phi, load_index, damping, frequency, gains, shapes):
    owned = damping.shape[0]
    steps = loads.shape[0]
    rows_here = phi.shape[0]
    local_index = load_index - lax.axis_index("dof") * rows_here
    selected = jnp.take(phi, local_index, axis=0)
    columns = lax.all_to_all(selected, "dof", split_axis=1, concat_axis=0, tiled=True)
    block = columns
    modal = lax.dot_general(
        block,
        lax.all_gather(loads, "dof", axis=1, tiled=True),
        (((0,), (1,)), ((), ())),
        preferred_element_type=jnp.float32,
    )
    drive = jnp.sqrt(-jnp.expm1(-2.0 * damping))
    width = min(128, steps)
    blocks = steps // width
    log_gain = jnp.cumsum(jnp.log(gains).reshape(blocks, width), axis=1)
    rise = jnp.exp(log_gain)
    fall = jnp.exp(-log_gain)
    offsets = jnp.arange(width, dtype=jnp.float32)
    lag = offsets[:, None] - offsets[None, :]
    lower = lag >= 0.0
    lag_pos = jnp.where(lower, lag, 0.0)
    decay = jnp.exp(-damping[:, None, None] * lag_pos[None, :, :])
    turn = frequency[:, None, None] * lag_pos[None, :, :]
    kernel_re = jnp.where(lower[None, :, :], decay * jnp.cos(turn), 0.0)
    kernel_im = jnp.where(lower[None, :, :], decay * jnp.sin(turn), 0.0)
    pushed = (drive[:, None] * modal).reshape(owned, blocks, width) * fall[None, :, :]
    local_re = (
        jnp.einsum("mts,mns->mnt", kernel_re, pushed, precision=lax.Precision.HIGHEST)
        * rise[None, :, :]
    )
    local_im = (
        jnp.einsum("mts,mns->mnt", kernel_im, pushed, precision=lax.Precision.HIGHEST)
        * rise[None, :, :]
    )
    ahead = offsets + 1.0
    power_mag = jnp.exp(-damping[:, None] * ahead[None, :])
    power_re = power_mag * jnp.cos(frequency[:, None] * ahead[None, :])
    power_im = power_mag * jnp.sin(frequency[:, None] * ahead[None, :])
    carry_re_all = power_re[:, None, :] * rise[None, :, :]
    carry_im_all = power_im[:, None, :] * rise[None, :, :]
    unit = jnp.ones((owned,), jnp.float32)
    nothing = jnp.zeros((owned,), jnp.float32)
    running = (unit, nothing, nothing, nothing)
    entering = []
    for index in range(blocks):
        entering.append(running)
        piece = (
            carry_re_all[:, index, width - 1],
            carry_im_all[:, index, width - 1],
            local_re[:, index, width - 1],
            local_im[:, index, width - 1],
        )
        running = combine(running, piece)
    incoming = carried_in(running, "tm", combine, (unit, nothing, nothing, nothing))
    state_re = []
    state_im = []
    for index in range(blocks):
        joined = combine(incoming, entering[index])
        state_re.append(joined[2])
        state_im.append(joined[3])
    enter_re = jnp.stack(state_re, axis=1)
    enter_im = jnp.stack(state_im, axis=1)
    history = (
        carry_re_all * enter_re[:, :, None] - carry_im_all * enter_im[:, :, None] + local_re
    ).reshape(owned, steps)
    rounded = history.astype(jnp.bfloat16)
    block = shapes
    field = lax.dot_general(
        lax.all_gather(rounded, "dof", axis=0, tiled=True),
        block,
        (((0,), (0,)), ((), ())),
        preferred_element_type=jnp.float32,
    )
    return (field.astype(jnp.bfloat16), history)


def solution(mesh):
    placed = (P("tm", "dof"), P("dof", None), P("dof"), P("dof"), P("dof"), P("tm"), P(None, "dof"))
    return jax.shard_map(
        body,
        mesh=mesh,
        in_specs=placed,
        out_specs=(P("tm", "dof"), P("dof", "tm")),
        check_vma=False,
    )
```

profile of v0, /device:TPU:0, one launch (start us, length us, event | category | flops | bytes accessed | tf_op | source)
XLA Modules:
  0.0 556.4 jit_solution(11666836741190187716)
XLA Ops:
  7.2 0.0 all-gather.7.cloned.1.call-start
  7.2 0.7 all-gather.7.cloned.1.call-update
  7.9 0.7 compare_and_fusion
  8.6 12.2 %gather_fusion = bf16[512,4096]{1,0:T(8,128)(2,1)} fusion(bf16[768,4096]{1,0:T(8,128)(2,1)} %param.10, s32[1024]{0:T(1024)S(1)} %pad_clamp_fusion), kind=kCustom, calls=%fused_computation | custom fusion | bytes 8390656 | tf_op jit(solution)/shard_map/jit(_take)/gather | solution.py:37
  20.8 0.0 copy-start.2
  20.8 0.0 copy-start.1
  20.8 0.0 copy-start
  20.8 4.7 bitcast_select_fusion
  25.4 5.1 all-to-all-start
  30.6 0.3 all-gather.9.cloned.1.call-start
  30.9 0.0 copy-done.2
  30.9 0.3 reduce_window_sum.11
  31.3 0.0 copy-done.1
  31.3 0.0 copy-done
  31.4 1.0 fusion.28
  32.4 0.4 broadcast_multiply_fusion.1
  32.8 12.6 %slice_reduce_fusion.6 = (f32[512]{0:T(512)S(1)}, f32[512]{0:T(512)S(1)}, f32[512]{0:T(512)S(1)}, f32[512]{0:T(512)S(1)}, f32[512]{0:T(512)S(1)}, /*index=5*/f32[512]{0:T(512)S(1)}) fusion(f32[512,3,128]{2,1,0:T(4,128)S(1)} %get-tuple-element.237, f32[512,3,128]{2,1,0:T(4,128)S(1)} %get-tuple-element.236), kind=kLoop, calls=%fused_computation.48 | loop fusion | bytes 24576 | tf_op jit(solution)/shard_map/slice | solution.py:83
  45.3 42.9 %all-to-all-done = bf16[512,8,512]{2,0,1:T(8,128)(2,1)} async-done(((bf16[512,8,512]{2,0,1:T(8,128)(2,1)}), bf16[512,8,512]{2,0,1:T(8,128)(2,1)}, u32[]{:S(2)}, u32[]{:S(2)}) %all-to-all-start) | async-done | bytes 4194336 | tf_op jit(solution)/shard_map/all_to_all | solution.py:38
  88.2 0.0 all-gather.7.cloned.1.call-done
  88.2 4.9 convolution_multiply_fusion
  93.2 0.4 copy.17
  93.5 174.0 %fusion.21 = f32[512,3,128]{2,1,0:T(4,128)S(1)} fusion(f32[512]{0:T(512)S(1)} %copy-done, f32[128,128]{1,0:T(8,128)S(1)} %fusion.30, f32[512]{0:T(512)S(1)} %get-tuple-element.241, pred[128,128]{1,0:T(8,128)(4,1)S(1)} %fusion.31, f32[512,3,128]{2,1,0:T(4,128)S(1)} %copy.17, f32[3,128]{1,0:T(4,128)S(1)} %get-tuple-element.239, ...), kind=kOutput, calls=%fused_computation.29 | convolution fusion | flops 335937536 | bytes 1661952 | tf_op jit(solution)/shard_map/mts,mns->mnt/dot_general | solution.py:62
  267.6 175.4 %fusion.18 = f32[512,3,128]{2,1,0:T(4,128)S(1)} fusion(f32[512]{0:T(512)S(1)} %copy-done, f32[128,128]{1,0:T(8,128)S(1)} %fusion.30, f32[512]{0:T(512)S(1)} %get-tuple-element.241, pred[128,128]{1,0:T(8,128)(4,1)S(1)} %fusion.31, f32[512,3,128]{2,1,0:T(4,128)S(1)} %copy.17, f32[3,128]{1,0:T(4,128)S(1)} %get-tuple-element.239, ...), kind=kOutput, calls=%fused_computation.28 | convolution fusion | flops 335937536 | bytes 1661952 | tf_op jit(solution)/shard_map/mts,mns->mnt/dot_general | solution.py:66
  443.0 12.5 %slice_reduce_fusion = (f32[512]{0:T(512)S(1)}, f32[512]{0:T(512)S(1)}, f32[512]{0:T(512)S(1)}, f32[512]{0:T(512)S(1)}, f32[512]{0:T(512)S(1)}, /*index=5*/f32[512]{0:T(512)S(1)}) fusion(f32[512,3,128]{2,1,0:T(4,128)S(1)} %fusion.18, f32[512,3,128]{2,1,0:T(4,128)S(1)} %fusion.21), kind=kLoop, calls=%fused_computation.42 | loop fusion | bytes 24576 | tf_op jit(solution)/shard_map/slice | solution.py:85
  455.6 12.8 %all-gather.2 = f32[4,1,512]{2,1,0:T(1,128)S(1)} all-gather(f32[1,1,512]{2,1,0:T(1,128)S(1)} %get-tuple-element.234), channel_id=1, replica_groups=mesh['tm'=4,'dof'=8] {'tm'}, dimensions={0}, use_global_device_ids=true | all-gather | bytes 10240 | tf_op jit(solution)/shard_map/all_gather | solution.py:9
  468.5 11.9 %all-gather = f32[4,1,512]{2,1,0:T(1,128)S(1)} all-gather(f32[1,1,512]{2,1,0:T(1,128)S(1)} %get-tuple-element.235), channel_id=1, replica_groups=mesh['tm'=4,'dof'=8] {'tm'}, dimensions={0}, use_global_device_ids=true | all-gather | bytes 10240 | tf_op jit(solution)/shard_map/all_gather | solution.py:9
  480.3 11.9 %all-gather.3 = f32[4,1,512]{2,1,0:T(1,128)S(1)} all-gather(f32[1,1,512]{2,1,0:T(1,128)S(1)} %get-tuple-element.209), channel_id=1, replica_groups=mesh['tm'=4,'dof'=8] {'tm'}, dimensions={0}, use_global_device_ids=true | all-gather | bytes 10240 | tf_op jit(solution)/shard_map/all_gather | solution.py:9
  492.2 11.9 %all-gather.1 = f32[4,1,512]{2,1,0:T(1,128)S(1)} all-gather(f32[1,1,512]{2,1,0:T(1,128)S(1)} %get-tuple-element.223), channel_id=1, replica_groups=mesh['tm'=4,'dof'=8] {'tm'}, dimensions={0}, use_global_device_ids=true | all-gather | bytes 10240 | tf_op jit(solution)/shard_map/all_gather | solution.py:9
  504.0 0.5 while.16
  504.6 0.1 copy.18
  504.8 0.1 copy.19
  504.9 1.4 subtract_add_fusion
  506.3 0.3 copy.20
  506.6 0.8 bitcast_convert_fusion
  507.4 0.0 all-gather.9.cloned.1.call-update
  507.4 1.1 copy.21
  508.6 28.5 %all-gather.9.cloned.1.call-done = bf16[4096,384]{0,1:T(8,128)(2,1)} async-done(((bf16[512,384]{0,1:T(8,128)(2,1)}), bf16[4096,384]{0,1:T(8,128)(2,1)}) %all-gather.9.cloned.1.call-update) | async-done | bytes 3145744 | tf_op jit(solution)/shard_map/all_gather | solution.py:103
  537.1 12.0 %convolution_convert_fusion = bf16[384,2048]{1,0:T(8,128)(2,1)} fusion(bf16[4096,384]{0,1:T(8,128)(2,1)} %all-gather.9.cloned.1.call-done, bf16[4096,2048]{1,0:T(8,128)(2,1)} %param.15), kind=kOutput, calls=%fused_computation.27 | convolution fusion | flops 6443237376 | bytes 21495808 | tf_op jit(solution)/shard_map/dot_general | solution.py:102
  (29 shorter events, 0.3 us)
Async XLA Ops:
  7.2 81.1 %all-gather.7.cloned.1.call-start = ((), (), s32[]{:S(2)}) async-start(), calls=%async_computation.1 | async-start | bytes 3538944 | tf_op jit(solution)/shard_map/all_gather | solution.py:42
  20.8 10.1 %copy-start.2 = (f32[384]{0:T(512)S(1)}, f32[384]{0:T(512)}, u32[]{:S(2)}) copy-start(f32[384]{0:T(512)} %param.14) | copy-start | bytes 4612
  20.8 10.5 %copy-start.1 = (f32[512]{0:T(512)S(1)}, f32[512]{0:T(512)}, u32[]{:S(2)}) copy-start(f32[512]{0:T(512)} %param.12) | copy-start | bytes 6148
  20.8 10.6 %copy-start = (f32[512]{0:T(512)S(1)}, f32[512]{0:T(512)}, u32[]{:S(2)}) copy-start(f32[512]{0:T(512)} %param.13) | copy-start | bytes 6148
  25.4 62.8 %all-to-all-start = ((bf16[512,8,512]{2,0,1:T(8,128)(2,1)}), bf16[512,8,512]{2,0,1:T(8,128)(2,1)}, u32[]{:S(2)}, u32[]{:S(2)}) async-start(bf16[512,8,512]{2,0,1:T(8,128)(2,1)} %bitcast_select_fusion), calls=%async_computation | async-start | bytes 8388608 | tf_op jit(solution)/shard_map/all_to_all | solution.py:38
  30.6 506.5 %all-gather.9.cloned.1.call-start = ((), (), s32[]{:S(2)}) async-start(), calls=%async_computation.2 | async-start | bytes 3538944 | tf_op jit(solution)/shard_map/all_gather | solution.py:103
Sparse Core Ops, SparseCore 0:
  9.9 43.9 all-gather.6
  507.6 29.4 all-gather.8
where the time goes:
time: 561 us; the launch traced here: 556 us
  matrix products  366 us (65%)
  waiting for transfers between devices  72.1 us (13%)
  blocking collectives  48.4 us (9%)
  local copies, waits for them, and re-layouts  39.5 us (7%)
  between operations  14.7 us (3%)
  other arithmetic  9.5 us (2%)
    dot_general x1, matrix products, body(): jnp.einsum('mts,mns->mnt', kernel_im, pushed, precision=lax.Precision.HIG...  175 us
    dot_general x1, matrix products, body(): jnp.einsum('mts,mns->mnt', kernel_re, pushed, precision=lax.Precision.HIG...  174 us
    all_gather x4, blocking collectives, carried_in(): pieces = jax.tree.map(lambda part: lax.all_gather(part, axis), value)  48.4 us
    all_to_all x1, waiting for transfers between devices, body(): lax.all_to_all(selected, 'dof', split_axis=1, concat_axis=0, tiled=True)  42.9 us
    all_gather x1, waiting for transfers between devices, body(): lax.all_gather(rounded, 'dof', axis=0, tiled=True)  28.5 us
    slice x1, local copies, waits for them, and re-layouts, body(): carry_im_all[:, index, width - 1]  12.6 us
    slice x1, local copies, waits for them, and re-layouts, body(): local_im[:, index, width - 1]  12.5 us
    gather x1, local copies, waits for them, and re-layouts, body(): selected = jnp.take(phi, local_index, axis=0)  12.2 us
  transfers between devices with their start and end apart: 3, of which 2 were waited for; matrix products, arithmetic and copies ran while one was open for 6% of the time, Pallas kernels for 0%

commit v1 on v0

--- a/solution.py
+++ b/solution.py
@@ -1,7 +1,435 @@
+import functools
+
 import jax
 import jax.numpy as jnp
 from jax import lax
+from jax.experimental import pallas as pl
+from jax.experimental.pallas import tpu as pltpu
 from jax.sharding import PartitionSpec as P
+
+MESH = pl.DeviceIdType.MESH
+NSUB = 2
+SEGS = 8
+CORE, DA, DB, XA, XB, YA, YB = 0, 4, 5, 6, 7, 8, 9
+GXA, GXB, GYA, GYB, GP, FA, FB, PX, PY, PD, TM = 10, 11, 12, 13, 14, 15, 16, 17, 18, 19, 20
+
+
+def cmul(ar, ai, br, bi):
+    return ar * br - ai * bi, ar * bi + ai * br
+
+
+def power(ar, ai, exponent):
+    result = None
+    while exponent:
+        if exponent & 1:
+            result = (ar, ai) if result is None else cmul(*result, ar, ai)
+        exponent >>= 1
+        if exponent:
+            ar, ai = cmul(ar, ai, ar, ai)
+    return result
+
+
+def kernel(
+    tms, pars, gains, index, loads, phi, shapes, field, hist,
+    onehot, spread, phi_buf, shapes_buf, tx_core, rx_core, tx_d, tx_x, tx_y, rx_d, rx_x, rx_y,
+    hold_x, hold_y, mod, tx_tm, rx_tm, carry, gath, acc, send, recv, phi_sem, shapes_sem,
+):
+    steps = loads.shape[0]
+    half = steps // 2
+    owned = pars.shape[1]
+    width = owned // NSUB
+    cols = width // 128
+    seg = steps // SEGS
+    rows = phi.shape[0]
+    channels = loads.shape[1]
+    points = shapes.shape[1]
+    tile = min(512, points)
+    top, low = pl.ds(0, half), pl.ds(half, half)
+
+    d = lax.axis_index("dof")
+    me = lax.axis_index("tm")
+    core = lax.rem(d, 2)
+    px = lax.rem(d // 2, 2)
+    py = d // 4
+    other = 1 - core
+    partner = d + 1 - 2 * core
+    xn = d + 2 * (1 - 2 * px)
+    yn = d + 4 * (1 - 2 * py)
+
+    def owner(q, cc):
+        fx, fy = q % 2, q // 2
+        x = px + fx * (1 - 2 * px)
+        y = py + fy * (1 - 2 * py)
+        return (y * 2 + x) * 2 + cc
+
+    def remote(src, dst, kind, s, to):
+        return pltpu.make_async_remote_copy(
+            src_ref=src, dst_ref=dst, send_sem=send.at[s, kind], recv_sem=recv.at[s, kind],
+            device_id={"dof": to}, device_id_type=MESH,
+        )
+
+    def core_copy(q, s):
+        return remote(tx_core.at[q, s], rx_core.at[q, s], CORE + q, s, partner)
+
+    def piece(src, dst, span, kind, s, to):
+        return remote(src.at[s, span], dst.at[s, span], kind, s, to)
+
+    def da(s):
+        return piece(tx_d, rx_d, top, DA, s, xn)
+
+    def db(s):
+        return piece(tx_d, rx_d, low, DB, s, yn)
+
+    def xa(s):
+        return piece(tx_x, rx_x, top, XA, s, xn)
+
+    def xb(s):
+        return piece(tx_x, rx_x, low, XB, s, xn)
+
+    def ya(s):
+        return piece(tx_y, rx_y, top, YA, s, yn)
+
+    def yb(s):
+        return piece(tx_y, rx_y, low, YB, s, yn)
+
+    def gathered(src, dst, span, kind, s, to):
+        return remote(gath.at[src[0], src[1], s, span], gath.at[dst[0], dst[1], s, span], kind, s, to)
+
+    whole = pl.ds(0, steps)
+
+    def gxa(s):
+        return gathered((0, 0), (1, 0), top, GXA, s, xn)
+
+    def gxb(s):
+        return gathered((0, 0), (1, 0), low, GXB, s, xn)
+
+    def gya(s):
+        return gathered((0, 0), (2, 0), top, GYA, s, yn)
+
+    def gyb(s):
+        return gathered((0, 0), (2, 0), low, GYB, s, yn)
+
+    def gp(s):
+        return gathered((0, 0), (0, 1), whole, GP, s, partner)
+
+    def fa(s):
+        return gathered((1, 0), (3, 0), top, FA, s, yn)
+
+    def fb(s):
+        return gathered((2, 0), (3, 0), low, FB, s, xn)
+
+    def pq(q, s):
+        return gathered((q, 0), (q, 1), whole, PX + q - 1, s, partner)
+
+    def state_copy(dk, s, to):
+        return pltpu.make_async_remote_copy(
+            src_ref=tx_tm.at[s], dst_ref=rx_tm.at[dk - 1, s],
+            send_sem=send.at[s, TM + dk - 1], recv_sem=recv.at[s, TM + dk - 1],
+            device_id={"tm": to}, device_id_type=MESH,
+        )
+
+    def phi_copy(slot, q, cc, s):
+        start = pl.multiple_of(owner(q, cc) * owned + s * width, width)
+        return pltpu.make_async_copy(phi.at[:, pl.ds(start, width)], phi_buf.at[slot], phi_sem.at[slot])
+
+    order = (3, 1, 2, 0)
+
+    def start_partner_tiles(s):
+        for slot in range(4):
+            phi_copy(slot, 3 - slot, other, s).start()
+
+    def start_own_tiles(s):
+        for slot, q in enumerate(order):
+            phi_copy(4 + slot, q, core, s).start()
+
+    shapes_copy = pltpu.make_async_copy(shapes, shapes_buf, shapes_sem)
+
+    barrier = pltpu.get_barrier_semaphore()
+    start_partner_tiles(0)
+    start_own_tiles(0)
+    for to in (partner, xn, yn):
+        pl.semaphore_signal(barrier, inc=1, device_id={"dof": to}, device_id_type=MESH)
+    for dk in range(1, tms):
+        to = lax.rem(me + dk, tms)
+        pl.semaphore_signal(barrier, inc=1, device_id={"tm": to}, device_id_type=MESH)
+
+    place = lax.broadcasted_iota(jnp.int32, (rows, channels), 0)
+    hit = jnp.where(place == index[...] - d * rows, 1.0, 0.0).astype(jnp.float32)
+    onehot[...] = hit.T.astype(jnp.bfloat16)
+    spread[...] = jnp.broadcast_to(gains[...], (128, steps)).T
+    pl.semaphore_wait(barrier, 3 + tms - 1)
+
+    def partial_modal(slot):
+        chosen = jnp.dot(onehot[...], phi_buf[slot], preferred_element_type=jnp.float32)
+        return jnp.dot(loads[...], chosen.astype(jnp.bfloat16), preferred_element_type=jnp.float32)
+
+    def for_partner(s):
+        def one(slot, _):
+            q = 3 - slot
+            phi_copy(slot, q, other, s).wait()
+            tx_core[q, s] = partial_modal(slot).astype(jnp.bfloat16)
+            core_copy(q, s).start()
+            return 0
+
+        lax.fori_loop(0, 4, one, 0)
+
+    def own_sum(slot, q, s):
+        phi_copy(4 + slot, q, core, s).wait()
+        value = partial_modal(4 + slot)
+        core_copy(q, s).wait_recv()
+        return value + rx_core[q, s].astype(jnp.float32)
+
+    def for_chips(s):
+        tx_d[s] = own_sum(0, 3, s).astype(jnp.bfloat16)
+        da(s).start()
+        db(s).start()
+        value = own_sum(1, 1, s)
+        tx_x[s, :half] = value[:half].astype(jnp.bfloat16)
+        xa(s).start()
+        hold_x[s] = value[half:]
+        value = own_sum(2, 2, s)
+        tx_y[s, half:] = value[half:].astype(jnp.bfloat16)
+        yb(s).start()
+        hold_y[s] = value[:half]
+        value = own_sum(3, 0, s)
+        for j in range(cols):
+            mod[s, j] = value[:, j * 128:(j + 1) * 128]
+
+    def pass_on(s):
+        db(s).wait_recv()
+        tx_x[s, half:] = (hold_x[s] + rx_d[s, half:].astype(jnp.float32)).astype(jnp.bfloat16)
+        xb(s).start()
+        da(s).wait_recv()
+        tx_y[s, :half] = (hold_y[s] + rx_d[s, :half].astype(jnp.float32)).astype(jnp.bfloat16)
+        ya(s).start()
+
+    def par(s, j):
+        lanes = slice(s * width + j * 128, s * width + (j + 1) * 128)
+        return pars[0:1, lanes], pars[1:2, lanes], pars[2:3, lanes]
+
+    def scan(s, start, store):
+        coefs = [tuple(jnp.broadcast_to(v, (SEGS, 128)) for v in par(s, j)[:2]) for j in range(cols)]
+
+        def step(i, state):
+            total, waves = state
+            at = pl.ds(i, SEGS, stride=seg)
+            gain = spread[at, :]
+            out = []
+            for j in range(cols):
+                re, im = cmul(*coefs[j], *waves[j])
+                re = gain * re + mod[s, j, at, :]
+                im = gain * im
+                if store:
+                    mod[s, j, at, :] = re
+                out.append((re, im))
+            return total * gain, tuple(out)
+
+        one = jnp.ones((SEGS, 128), jnp.float32)
+        return lax.fori_loop(0, seg, step, (one, tuple(start)), unroll=8)
+
+    def local_states(s):
+        for copy in (xa(s), xb(s), ya(s), yb(s)):
+            copy.wait_recv()
+        for j in range(cols):
+            lanes = slice(j * 128, (j + 1) * 128)
+            value = mod[s, j] + rx_x[s, :, lanes].astype(jnp.float32) + rx_y[s, :, lanes].astype(jnp.float32)
+            mod[s, j] = value * par(s, j)[2]
+        zero = jnp.zeros((SEGS, 128), jnp.float32)
+        total, ends = scan(s, [(zero, zero)] * cols, False)
+        kept = []
+        for j in range(cols):
+            lanes = slice(j * 128, (j + 1) * 128)
+            a, b, _ = par(s, j)
+            ar, ai = power(a, b, seg)
+            state = (jnp.zeros((1, 128), jnp.float32),) * 2
+            prod = (jnp.ones((1, 128), jnp.float32), jnp.zeros((1, 128), jnp.float32))
+            entering, products = [], []
+            gain = jnp.ones((1, 128), jnp.float32)
+            for k in range(SEGS):
+                entering.append(state)
+                products.append(prod)
+                g = total[k:k + 1]
+                c = (ar * g, ai * g)
+                moved = cmul(*c, *state)
+                state = (moved[0] + ends[j][0][k:k + 1], moved[1] + ends[j][1][k:k + 1])
+                prod = cmul(*c, *prod)
+                gain = gain * g
+            tx_tm[s, 0:1, lanes] = state[0]
+            tx_tm[s, 1:2, lanes] = state[1]
+            tx_tm[s, 2:3, lanes] = gain
+            kept.append(tuple(
+                jnp.concatenate([v[n] for v in some], axis=0) for some in (entering, products) for n in (0, 1)
+            ))
+        for dk in range(1, tms):
+            @pl.when(me + dk < tms)
+            def _():
+                state_copy(dk, s, me + dk).start()
+        return kept
+
+    def finish(s, kept):
+        carry[s] = jnp.zeros(carry.shape[1:], jnp.float32)
+        for dk in range(tms - 1, 0, -1):
+            @pl.when(me >= dk)
+            def _():
+                state_copy(dk, s, me).wait_recv()
+                for j in range(cols):
+                    lanes = slice(j * 128, (j + 1) * 128)
+                    a, b, _ = par(s, j)
+                    ar, ai = power(a, b, steps)
+                    gain = rx_tm[dk - 1, s, 2:3, lanes]
+                    re, im = cmul(ar * gain, ai * gain, carry[s, 0:1, lanes], carry[s, 1:2, lanes])
+                    carry[s, 0:1, lanes] = re + rx_tm[dk - 1, s, 0:1, lanes]
+                    carry[s, 1:2, lanes] = im + rx_tm[dk - 1, s, 1:2, lanes]
+        start = []
+        for j in range(cols):
+            lanes = slice(j * 128, (j + 1) * 128)
+            er, ei, kr, ki = kept[j]
+            re, im = cmul(kr, ki, carry[s, 0:1, lanes], carry[s, 1:2, lanes])
+            start.append((er + re, ei + im))
+        scan(s, start, True)
+        for j in range(cols):
+            gath[0, 0, s, :, j * 128:(j + 1) * 128] = mod[s, j].astype(jnp.bfloat16)
+        for copy in (gxa(s), gyb(s), gp(s), gxb(s), gya(s)):
+            copy.start()
+        for j in range(cols):
+            hist[s * width + j * 128:s * width + (j + 1) * 128, :] = mod[s, j].T
+
+    def forward(s):
+        gxa(s).wait_recv()
+        fa(s).start()
+        gyb(s).wait_recv()
+        fb(s).start()
+
+    def share(s):
+        gxb(s).wait_recv()
+        pq(1, s).start()
+        gya(s).wait_recv()
+        pq(2, s).start()
+
+    def share_last(s):
+        fa(s).wait_recv()
+        fb(s).wait_recv()
+        pq(3, s).start()
+
+    def expand(q, s, mode):
+        mine = pl.multiple_of(owner(q, core) * owned + s * width, width)
+        theirs = pl.multiple_of(owner(q, other) * owned + s * width, width)
+
+        def one(n, _):
+            at = pl.ds(pl.multiple_of(n * tile, tile), tile)
+            value = jnp.dot(gath[q, 0, s], shapes_buf[pl.ds(mine, width), at], preferred_element_type=jnp.float32)
+            value += jnp.dot(gath[q, 1, s], shapes_buf[pl.ds(theirs, width), at], preferred_element_type=jnp.float32)
+            if mode != "first":
+                value += acc[:, at]
+            if mode == "last":
+                field[:, at] = value.astype(jnp.bfloat16)
+            else:
+                acc[:, at] = value
+            return 0
+
+        lax.fori_loop(0, points // tile, one, 0)
+
+    for_partner(0)
+    start_partner_tiles(1)
+    for_chips(0)
+    start_own_tiles(1)
+    shapes_copy.start()
+    for_partner(1)
+    pass_on(0)
+    for_chips(1)
+    kept_0 = local_states(0)
+    pass_on(1)
+    finish(0, kept_0)
+    kept_1 = local_states(1)
+    forward(0)
+    finish(1, kept_1)
+    share(0)
+    shapes_copy.wait()
+    gp(0).wait_recv()
+    expand(0, 0, "first")
+    forward(1)
+    share_last(0)
+    gp(1).wait_recv()
+    expand(0, 1, "add")
+    pq(1, 0).wait_recv()
+    expand(1, 0, "add")
+    share(1)
+    pq(2, 0).wait_recv()
+    expand(2, 0, "add")
+    pq(3, 0).wait_recv()
+    expand(3, 0, "add")
+    pq(1, 1).wait_recv()
+    expand(1, 1, "add")
+    share_last(1)
+    pq(2, 1).wait_recv()
+    expand(2, 1, "add")
+    pq(3, 1).wait_recv()
+    expand(3, 1, "last")
+
+    for s in range(NSUB):
+        for q in range(4):
+            core_copy(q, s).wait_send()
+        for copy in (
+            da(s), db(s), xa(s), xb(s), ya(s), yb(s), gxa(s), gxb(s), gya(s), gyb(s), gp(s), fa(s), fb(s),
+            pq(1, s), pq(2, s), pq(3, s),
+        ):
+            copy.wait_send()
+        for dk in range(1, tms):
+            @pl.when(me + dk < tms)
+            def _():
+                state_copy(dk, s, me).wait_send()
+
+
+def fused(tms, loads, phi, load_index, damping, frequency, gains, shapes):
+    owned, steps, channels = damping.shape[0], loads.shape[0], loads.shape[1]
+    rows, points, modes = phi.shape[0], shapes.shape[1], shapes.shape[0]
+    width = owned // NSUB
+    half = steps // 2
+    radius = jnp.exp(-damping)
+    drive = jnp.sqrt(-jnp.expm1(-2.0 * damping))
+    pars = jnp.stack([radius * jnp.cos(frequency), radius * jnp.sin(frequency), drive])
+    b16, f32 = jnp.bfloat16, jnp.float32
+    kinds = TM + tms - 1
+    small = pl.BlockSpec(memory_space=pltpu.VMEM)
+    large = pl.BlockSpec(memory_space=pl.ANY)
+    return pl.pallas_call(
+        functools.partial(kernel, tms),
+        out_shape=(
+            jax.ShapeDtypeStruct((steps, points), b16),
+            jax.ShapeDtypeStruct((owned, steps), f32),
+        ),
+        in_specs=[small, small, small, small, large, large],
+        out_specs=(small, small),
+        scratch_shapes=[
+            pltpu.VMEM((channels, rows), b16),
+            pltpu.VMEM((steps, 128), f32),
+            pltpu.VMEM((8, rows, width), b16),
+            pltpu.VMEM((modes, points), b16),
+            pltpu.VMEM((4, NSUB, steps, width), b16),
+            pltpu.VMEM((4, NSUB, steps, width), b16),
+        ] + [pltpu.VMEM((NSUB, steps, width), b16)] * 6 + [
+            pltpu.VMEM((NSUB, half, width), f32),
+            pltpu.VMEM((NSUB, half, width), f32),
+            pltpu.VMEM((NSUB, width // 128, steps, 128), f32),
+            pltpu.VMEM((NSUB, 8, width), f32),
+            pltpu.VMEM((tms - 1, NSUB, 8, width), f32),
+            pltpu.VMEM((NSUB, 8, width), f32),
+            pltpu.VMEM((4, 2, NSUB, steps, width), b16),
+            pltpu.VMEM((steps, points), f32),
+            pltpu.SemaphoreType.DMA((NSUB, kinds)),
+            pltpu.SemaphoreType.DMA((NSUB, kinds)),
+            pltpu.SemaphoreType.DMA((8,)),
+            pltpu.SemaphoreType.DMA,
+        ],
+        compiler_params=pltpu.CompilerParams(
+            collective_id=0, has_side_effects=True, vmem_limit_bytes=56 * 1024 * 1024
+        ),
+        cost_estimate=pl.CostEstimate(
+            flops=2 * steps * modes * (points + channels) + 2 * channels * rows * modes,
+            bytes_accessed=2 * (modes * points + rows * modes + steps * points),
+            transcendentals=0,
+        ),
+    )(pars, gains.reshape(1, steps), load_index.reshape(1, channels), loads, phi, shapes)
 
 
 def carried_in(value, axis, join, neutral):
@@ -110,8 +538,9 @@
 
 def solution(mesh):
     placed = (P("tm", "dof"), P("dof", None), P("dof"), P("dof"), P("dof"), P("tm"), P(None, "dof"))
+    part = functools.partial(fused, mesh.shape["tm"]) if mesh.shape["dof"] == 8 else body
     return jax.shard_map(
-        body,
+        part,
         mesh=mesh,
         in_specs=placed,
         out_specs=(P("tm", "dof"), P("dof", "tm")),

time: 561 us -> 57.2 us (0.10)
  matrix products: 366 us -> 0 us
  waiting for transfers between devices: 72.1 us -> 0 us
  Pallas kernels: 0 us -> 48.9 us
  blocking collectives: 48.4 us -> 0 us
  local copies, waits for them, and re-layouts: 39.5 us -> 6.04 us
  between operations: 14.7 us -> 0.64 us
  other arithmetic: 9.5 us -> 1.35 us
    dot_general x4 -> x0, matrix products: 366 us -> none  [the longest x1 175 us: body(): jnp.einsum('mts,mns->mnt', kernel_im, pushed, precision=lax.Precision.HIG...]
    pallas_call x0 -> x1, Pallas kernels: none -> 48.9 us  [fused(): pl.pallas_call(functools.partial(kernel, tms), out_shape=(jax.ShapeDtypeS...]
    all_gather x4 -> x0, blocking collectives: 48.4 us -> none  [carried_in(): pieces = jax.tree.map(lambda part: lax.all_gather(part, axis), value)]
    all_to_all x1 -> x0, waiting for transfers between devices: 42.9 us -> none  [body(): lax.all_to_all(selected, 'dof', split_axis=1, concat_axis=0, tiled=True)]
    all_gather x2 -> x0, waiting for transfers between devices: 28.5 us -> none  [the longest x1 28.5 us: body(): lax.all_gather(rounded, 'dof', axis=0, tiled=True)]
    slice x2 -> x0, local copies, waits for them, and re-layouts: 25.1 us -> none  [the longest x1 12.6 us: body(): carry_im_all[:, index, width - 1]]
    gather x1 -> x0, local copies, waits for them, and re-layouts: 12.2 us -> none  [body(): selected = jnp.take(phi, local_index, axis=0)]
  transfers between devices with their start and end apart: 3 -> 0, of which waited for: 2 -> 0; matrix products, arithmetic and copies ran while one was open for 6% -> 0% of each run, Pallas kernels for 0% -> 0%
where the time goes in v1:
time: 57.2 us; the launch traced here: 57 us
  Pallas kernels  48.9 us (85%)
  local copies, waits for them, and re-layouts  6.04 us (11%)
  other arithmetic  1.35 us (2%)
  between operations  0.64 us (1%)
    pallas_call x1, Pallas kernels, fused(): pl.pallas_call(functools.partial(kernel, tms), out_shape=(jax.ShapeDtypeS...  48.9 us
    unnamed x2, local copies, waits for them, and re-layouts  4.79 us
    reshape x1, local copies, waits for them, and re-layouts, fused(): gains.reshape(1, steps)  1.25 us

profile of v1, /device:TPU:0, one launch (start us, length us, event | category | flops | bytes accessed | tf_op | source)
XLA Modules:
  0.0 57.0 jit_solution(11156659349483420799)
XLA Ops:
  0.6 1.2 %reshape.10.gains = f32[1,384]{1,0:T(1,128)} reshape(f32[384]{0:T(512)} %param.12) | data formatting | bytes 3072 | tf_op jit(solution)/shard_map/reshape | solution.py:432
  1.9 0.7 %cosine_multiply_fusion = (f32[512]{0:T(512)S(1)}, f32[512]{0:T(512)S(1)}, f32[512]{0:T(512)S(1)}) fusion(f32[512]{0:T(512)} %param.11, f32[512]{0:T(512)} %param.10), kind=kLoop, calls=%fused_computation.3 | loop fusion | flops 2560 | bytes 10240 | tf_op jit(solution)/shard_map/mul | solution.py:390
  2.6 0.6 %pad_maximum_fusion.pars = f32[3,512]{1,0:T(4,128)} fusion(f32[1,512]{1,0:T(1,128)S(1)} %bitcast.6, f32[1,512]{1,0:T(1,128)S(1)} %bitcast.5, f32[1,512]{1,0:T(1,128)S(1)} %bitcast.4), kind=kLoop, calls=%fused_computation | loop fusion | flops 3072 | bytes 12288 | tf_op jit(solution)/shard_map/stack | solution.py:390
  3.2 48.9 %shard_map.86 = (bf16[384,2048]{1,0:T(8,128)(2,1)}, f32[512,384]{1,0:T(8,128)}) custom-call(f32[3,512]{1,0:T(4,128)} %pad_maximum_fusion.pars, f32[1,384]{1,0:T(1,128)} %reshape.10.gains, s32[1,512]{1,0:T(1,128)} %bitcast.7, bf16[384,512]{1,0:T(8,128)(2,1)} %loads.1, bf16[768,4096]{1,0:T(8,128)(2,1)} %phi.1, bf16[4096,2048]{1,0:T(8,128)(2,1)} %shapes.1), custom_call_target="tpu_custom_call" | custom-call | flops 11274289152 | bytes 24641536 | tf_op jit(solution)/shard_map/pallas_call | solution.py:395
  52.2 2.7 %copy.11 = bf16[384,2048]{1,0:T(8,128)(2,1)} copy(bf16[384,2048]{1,0:T(8,128)(2,1)} %get-tuple-element.7) | data formatting | bytes 3145728
  54.9 2.1 %copy.12 = f32[512,384]{1,0:T(8,128)} copy(f32[512,384]{1,0:T(8,128)} %get-tuple-element.8) | data formatting | bytes 1572864

commit v2 on v1

--- a/solution.py
+++ b/solution.py
@@ -30,9 +30,10 @@
 
 
 def kernel(
-    tms, pars, gains, index, loads, phi, shapes, field, hist,
-    onehot, spread, phi_buf, shapes_buf, tx_core, rx_core, tx_d, tx_x, tx_y, rx_d, rx_x, rx_y,
-    hold_x, hold_y, mod, tx_tm, rx_tm, carry, gath, acc, send, recv, phi_sem, shapes_sem,
+    tms, damping, frequency, gains, index, loads_in, phi, shapes, field, hist,
+    pars, onehot, spread, loads, phi_buf, shapes_buf, tx_core, rx_core, own, tx_d, tx_x, tx_y, rx_d, rx_x, rx_y,
+    mod, tx_tm, rx_tm, carry, gath, acc, turned, rounded,
+    send, recv, loads_sem, phi_sem, shapes_sem, turned_sem, field_sem,
 ):
     steps = loads.shape[0]
     half = steps // 2
@@ -92,8 +93,11 @@
     def yb(s):
         return piece(tx_y, rx_y, low, YB, s, yn)
 
+    def lanes_of(q, r, s):
+        return pl.ds(((s * 4 + q) * 2 + r) * width, width)
+
     def gathered(src, dst, span, kind, s, to):
-        return remote(gath.at[src[0], src[1], s, span], gath.at[dst[0], dst[1], s, span], kind, s, to)
+        return remote(gath.at[span, lanes_of(*src, s)], gath.at[span, lanes_of(*dst, s)], kind, s, to)
 
     whole = pl.ds(0, steps)
 
@@ -128,79 +132,93 @@
             device_id={"tm": to}, device_id_type=MESH,
         )
 
-    def phi_copy(slot, q, cc, s):
-        start = pl.multiple_of(owner(q, cc) * owned + s * width, width)
-        return pltpu.make_async_copy(phi.at[:, pl.ds(start, width)], phi_buf.at[slot], phi_sem.at[slot])
-
+    def phi_copy(q, r, s):
+        start = pl.multiple_of(owner(q, other if r else core) * owned + s * width, width)
+        return pltpu.make_async_copy(
+            phi.at[:, pl.ds(start, width)], phi_buf.at[s, q, r], phi_sem.at[s, q, r]
+        )
+
+    def shapes_copy(q, r, s):
+        start = pl.multiple_of(owner(q, other if r else core) * owned + s * width, width)
+        return pltpu.make_async_copy(
+            shapes.at[pl.ds(start, width), :], shapes_buf.at[lanes_of(q, r, s), :], shapes_sem.at[s, q, r]
+        )
+
+    loads_copy = pltpu.make_async_copy(loads_in, loads, loads_sem)
     order = (3, 1, 2, 0)
 
-    def start_partner_tiles(s):
-        for slot in range(4):
-            phi_copy(slot, 3 - slot, other, s).start()
-
-    def start_own_tiles(s):
-        for slot, q in enumerate(order):
-            phi_copy(4 + slot, q, core, s).start()
-
-    shapes_copy = pltpu.make_async_copy(shapes, shapes_buf, shapes_sem)
-
     barrier = pltpu.get_barrier_semaphore()
-    start_partner_tiles(0)
-    start_own_tiles(0)
     for to in (partner, xn, yn):
         pl.semaphore_signal(barrier, inc=1, device_id={"dof": to}, device_id_type=MESH)
     for dk in range(1, tms):
         to = lax.rem(me + dk, tms)
         pl.semaphore_signal(barrier, inc=1, device_id={"tm": to}, device_id_type=MESH)
-
-    place = lax.broadcasted_iota(jnp.int32, (rows, channels), 0)
-    hit = jnp.where(place == index[...] - d * rows, 1.0, 0.0).astype(jnp.float32)
-    onehot[...] = hit.T.astype(jnp.bfloat16)
-    spread[...] = jnp.broadcast_to(gains[...], (128, steps)).T
-    pl.semaphore_wait(barrier, 3 + tms - 1)
-
-    def partial_modal(slot):
-        chosen = jnp.dot(onehot[...], phi_buf[slot], preferred_element_type=jnp.float32)
+    loads_copy.start()
+    for s in range(NSUB):
+        for q in order:
+            phi_copy(q, 1, s).start()
+            phi_copy(q, 0, s).start()
+
+    names = jnp.broadcast_to(index[...] - d * rows, (128, channels)).T
+    for j in range(rows // 128):
+        place = lax.broadcasted_iota(jnp.int32, (channels, 128), 1) + j * 128
+        onehot[:, j * 128:(j + 1) * 128] = jnp.where(place == names, 1.0, 0.0).astype(jnp.bfloat16)
+    loads_copy.wait()
+
+    def partial_modal(q, r, s):
+        phi_copy(q, r, s).wait()
+        chosen = jnp.dot(onehot[...], phi_buf[s, q, r], preferred_element_type=jnp.float32)
         return jnp.dot(loads[...], chosen.astype(jnp.bfloat16), preferred_element_type=jnp.float32)
 
-    def for_partner(s):
-        def one(slot, _):
-            q = 3 - slot
-            phi_copy(slot, q, other, s).wait()
-            tx_core[q, s] = partial_modal(slot).astype(jnp.bfloat16)
-            core_copy(q, s).start()
-            return 0
-
-        lax.fori_loop(0, 4, one, 0)
-
-    def own_sum(slot, q, s):
-        phi_copy(4 + slot, q, core, s).wait()
-        value = partial_modal(4 + slot)
+    def for_partner(q, s):
+        tx_core[q, s] = partial_modal(q, 1, s).astype(jnp.bfloat16)
+        if q == order[0] and s == 0:
+            pl.semaphore_wait(barrier, 3 + tms - 1)
+        core_copy(q, s).start()
+
+    def chip_sum(q, s, span):
+        return own[s, q, span] + rx_core[q, s, span].astype(jnp.float32)
+
+    def to_chip(q, s):
         core_copy(q, s).wait_recv()
-        return value + rx_core[q, s].astype(jnp.float32)
-
-    def for_chips(s):
-        tx_d[s] = own_sum(0, 3, s).astype(jnp.bfloat16)
-        da(s).start()
-        db(s).start()
-        value = own_sum(1, 1, s)
-        tx_x[s, :half] = value[:half].astype(jnp.bfloat16)
-        xa(s).start()
-        hold_x[s] = value[half:]
-        value = own_sum(2, 2, s)
-        tx_y[s, half:] = value[half:].astype(jnp.bfloat16)
-        yb(s).start()
-        hold_y[s] = value[:half]
-        value = own_sum(3, 0, s)
-        for j in range(cols):
-            mod[s, j] = value[:, j * 128:(j + 1) * 128]
+        if q == 3:
+            tx_d[s] = chip_sum(q, s, pl.ds(0, steps)).astype(jnp.bfloat16)
+            da(s).start()
+            db(s).start()
+        if q == 1:
+            tx_x[s, top] = chip_sum(q, s, top).astype(jnp.bfloat16)
+            xa(s).start()
+        if q == 2:
+            tx_y[s, low] = chip_sum(q, s, low).astype(jnp.bfloat16)
+            yb(s).start()
+
+    def partials(s, between=None):
+        for n, q in enumerate(order):
+            for_partner(q, s)
+            if n:
+                to_chip(order[n - 1], s)
+            if between is not None and n == 2:
+                between()
+            own[s, q] = partial_modal(q, 0, s)
+
+    def parameters():
+        x = 2.0 * damping[...]
+        series = jnp.ones_like(x)
+        for n in range(12, 1, -1):
+            series = 1.0 - x * series / n
+        drive = jnp.sqrt(jnp.where(x < 0.5, x * series, 1.0 - jnp.exp(-x)))
+        radius = jnp.exp(-damping[...])
+        pars[0:1, :] = radius * jnp.cos(frequency[...])
+        pars[1:2, :] = radius * jnp.sin(frequency[...])
+        pars[2:3, :] = drive
+        spread[...] = jnp.broadcast_to(gains[...].reshape(1, steps), (128, steps)).T
 
     def pass_on(s):
         db(s).wait_recv()
-        tx_x[s, half:] = (hold_x[s] + rx_d[s, half:].astype(jnp.float32)).astype(jnp.bfloat16)
+        tx_x[s, low] = (chip_sum(1, s, low) + rx_d[s, low].astype(jnp.float32)).astype(jnp.bfloat16)
         xb(s).start()
         da(s).wait_recv()
-        tx_y[s, :half] = (hold_y[s] + rx_d[s, :half].astype(jnp.float32)).astype(jnp.bfloat16)
+        tx_y[s, top] = (chip_sum(2, s, top) + rx_d[s, top].astype(jnp.float32)).astype(jnp.bfloat16)
         ya(s).start()
 
     def par(s, j):
@@ -228,11 +246,13 @@
         return lax.fori_loop(0, seg, step, (one, tuple(start)), unroll=8)
 
     def local_states(s):
-        for copy in (xa(s), xb(s), ya(s), yb(s)):
+        for copy in (core_copy(0, s), xa(s), xb(s), ya(s), yb(s)):
             copy.wait_recv()
         for j in range(cols):
             lanes = slice(j * 128, (j + 1) * 128)
-            value = mod[s, j] + rx_x[s, :, lanes].astype(jnp.float32) + rx_y[s, :, lanes].astype(jnp.float32)
+            value = own[s, 0, :, lanes]
+            for part in (rx_core.at[0], rx_x, rx_y):
+                value += part[s, :, lanes].astype(jnp.float32)
             mod[s, j] = value * par(s, j)[2]
         zero = jnp.zeros((SEGS, 128), jnp.float32)
         total, ends = scan(s, [(zero, zero)] * cols, False)
@@ -288,11 +308,16 @@
             start.append((er + re, ei + im))
         scan(s, start, True)
         for j in range(cols):
-            gath[0, 0, s, :, j * 128:(j + 1) * 128] = mod[s, j].astype(jnp.bfloat16)
+            gath[:, pl.ds(s * 8 * width + j * 128, 128)] = mod[s, j].astype(jnp.bfloat16)
         for copy in (gxa(s), gyb(s), gp(s), gxb(s), gya(s)):
             copy.start()
         for j in range(cols):
-            hist[s * width + j * 128:s * width + (j + 1) * 128, :] = mod[s, j].T
+            turned[s * width + j * 128:s * width + (j + 1) * 128, :] = mod[s, j].T
+        turned_copy(s).start()
+
+    def turned_copy(s):
+        at = pl.ds(s * width, width)
+        return pltpu.make_async_copy(turned.at[at], hist.at[at], turned_sem.at[s])
 
     def forward(s):
         gxa(s).wait_recv()
@@ -311,61 +336,67 @@
         fb(s).wait_recv()
         pq(3, s).start()
 
-    def expand(q, s, mode):
-        mine = pl.multiple_of(owner(q, core) * owned + s * width, width)
-        theirs = pl.multiple_of(owner(q, other) * owned + s * width, width)
+    def field_copy(n):
+        at = pl.ds(pl.multiple_of(n * tile, tile), tile)
+        return pltpu.make_async_copy(rounded.at[:, at], field.at[:, at], field_sem.at[n])
+
+    def expand(first, count, mode):
+        for block in range(first, first + count):
+            s, q = block // 4, block % 4
+            shapes_copy(q, 0, s).wait()
+            shapes_copy(q, 1, s).wait()
+        deep = pl.ds(first * 2 * width, count * 2 * width)
 
         def one(n, _):
             at = pl.ds(pl.multiple_of(n * tile, tile), tile)
-            value = jnp.dot(gath[q, 0, s], shapes_buf[pl.ds(mine, width), at], preferred_element_type=jnp.float32)
-            value += jnp.dot(gath[q, 1, s], shapes_buf[pl.ds(theirs, width), at], preferred_element_type=jnp.float32)
+            value = jnp.dot(gath[:, deep], shapes_buf[deep, at], preferred_element_type=jnp.float32)
             if mode != "first":
                 value += acc[:, at]
             if mode == "last":
-                field[:, at] = value.astype(jnp.bfloat16)
+                rounded[:, at] = value.astype(jnp.bfloat16)
+                field_copy(n).start()
             else:
                 acc[:, at] = value
             return 0
 
         lax.fori_loop(0, points // tile, one, 0)
 
-    for_partner(0)
-    start_partner_tiles(1)
-    for_chips(0)
-    start_own_tiles(1)
-    shapes_copy.start()
-    for_partner(1)
-    pass_on(0)
-    for_chips(1)
+    partials(0)
+    for s in range(NSUB):
+        for q in range(4):
+            shapes_copy(q, 0, s).start()
+            shapes_copy(q, 1, s).start()
+    parameters()
+    partials(1, lambda: pass_on(0))
     kept_0 = local_states(0)
     pass_on(1)
     finish(0, kept_0)
     kept_1 = local_states(1)
+    gp(0).wait_recv()
+    expand(0, 1, "first")
     forward(0)
     finish(1, kept_1)
     share(0)
-    shapes_copy.wait()
-    gp(0).wait_recv()
-    expand(0, 0, "first")
+    share_last(0)
+    pq(1, 0).wait_recv()
+    pq(2, 0).wait_recv()
+    expand(1, 2, "add")
     forward(1)
-    share_last(0)
+    pq(3, 0).wait_recv()
     gp(1).wait_recv()
-    expand(0, 1, "add")
-    pq(1, 0).wait_recv()
-    expand(1, 0, "add")
+    expand(3, 2, "add")
     share(1)
-    pq(2, 0).wait_recv()
-    expand(2, 0, "add")
-    pq(3, 0).wait_recv()
-    expand(3, 0, "add")
+    share_last(1)
     pq(1, 1).wait_recv()
-    expand(1, 1, "add")
-    share_last(1)
     pq(2, 1).wait_recv()
-    expand(2, 1, "add")
+    expand(5, 2, "add")
     pq(3, 1).wait_recv()
-    expand(3, 1, "last")
-
+    expand(7, 1, "last")
+
+    for n in range(points // tile):
+        field_copy(n).wait()
+    for s in range(NSUB):
+        turned_copy(s).wait()
     for s in range(NSUB):
         for q in range(4):
             core_copy(q, s).wait_send()
@@ -380,46 +411,79 @@
                 state_copy(dk, s, me).wait_send()
 
 
+def hand_over(*arrays):
+    pieces = 4
+
+    def copies(*refs):
+        count = len(arrays)
+        started = []
+        for n in range(count):
+            rows = arrays[n].shape[0] // pieces
+            for piece in range(pieces):
+                at = pl.ds(piece * rows, rows)
+                started.append(
+                    pltpu.make_async_copy(refs[n].at[at], refs[count + n].at[at], refs[2 * count].at[n, piece])
+                )
+        for copy in started:
+            copy.start()
+        for copy in started:
+            copy.wait()
+
+    large = pl.BlockSpec(memory_space=pltpu.HBM)
+    return pl.pallas_call(
+        copies,
+        out_shape=tuple(jax.ShapeDtypeStruct(a.shape, a.dtype) for a in arrays),
+        in_specs=[large] * len(arrays),
+        out_specs=(large,) * len(arrays),
+        scratch_shapes=[pltpu.SemaphoreType.DMA((len(arrays), pieces))],
+        cost_estimate=pl.CostEstimate(
+            flops=0, bytes_accessed=sum(2 * a.size * a.dtype.itemsize for a in arrays), transcendentals=0
+        ),
+    )(*arrays)
+
+
 def fused(tms, loads, phi, load_index, damping, frequency, gains, shapes):
     owned, steps, channels = damping.shape[0], loads.shape[0], loads.shape[1]
     rows, points, modes = phi.shape[0], shapes.shape[1], shapes.shape[0]
     width = owned // NSUB
-    half = steps // 2
-    radius = jnp.exp(-damping)
-    drive = jnp.sqrt(-jnp.expm1(-2.0 * damping))
-    pars = jnp.stack([radius * jnp.cos(frequency), radius * jnp.sin(frequency), drive])
     b16, f32 = jnp.bfloat16, jnp.float32
     kinds = TM + tms - 1
     small = pl.BlockSpec(memory_space=pltpu.VMEM)
     large = pl.BlockSpec(memory_space=pl.ANY)
-    return pl.pallas_call(
+    results = pl.pallas_call(
         functools.partial(kernel, tms),
         out_shape=(
             jax.ShapeDtypeStruct((steps, points), b16),
             jax.ShapeDtypeStruct((owned, steps), f32),
         ),
-        in_specs=[small, small, small, small, large, large],
-        out_specs=(small, small),
+        in_specs=[small, small, small, small, large, large, large],
+        out_specs=(large, large),
         scratch_shapes=[
+            pltpu.VMEM((8, owned), f32),
             pltpu.VMEM((channels, rows), b16),
             pltpu.VMEM((steps, 128), f32),
-            pltpu.VMEM((8, rows, width), b16),
+            pltpu.VMEM((steps, channels), b16),
+            pltpu.VMEM((NSUB, 4, 2, rows, width), b16),
             pltpu.VMEM((modes, points), b16),
             pltpu.VMEM((4, NSUB, steps, width), b16),
             pltpu.VMEM((4, NSUB, steps, width), b16),
+            pltpu.VMEM((NSUB, 4, steps, width), f32),
         ] + [pltpu.VMEM((NSUB, steps, width), b16)] * 6 + [
-            pltpu.VMEM((NSUB, half, width), f32),
-            pltpu.VMEM((NSUB, half, width), f32),
             pltpu.VMEM((NSUB, width // 128, steps, 128), f32),
             pltpu.VMEM((NSUB, 8, width), f32),
             pltpu.VMEM((tms - 1, NSUB, 8, width), f32),
             pltpu.VMEM((NSUB, 8, width), f32),
-            pltpu.VMEM((4, 2, NSUB, steps, width), b16),
+            pltpu.VMEM((steps, modes), b16),
             pltpu.VMEM((steps, points), f32),
+            pltpu.VMEM((owned, steps), f32),
+            pltpu.VMEM((steps, points), b16),
             pltpu.SemaphoreType.DMA((NSUB, kinds)),
             pltpu.SemaphoreType.DMA((NSUB, kinds)),
-            pltpu.SemaphoreType.DMA((8,)),
             pltpu.SemaphoreType.DMA,
+            pltpu.SemaphoreType.DMA((NSUB, 4, 2)),
+            pltpu.SemaphoreType.DMA((NSUB, 4, 2)),
+            pltpu.SemaphoreType.DMA((NSUB,)),
+            pltpu.SemaphoreType.DMA((points // min(512, points),)),
         ],
         compiler_params=pltpu.CompilerParams(
             collective_id=0, has_side_effects=True, vmem_limit_bytes=56 * 1024 * 1024
@@ -429,7 +493,8 @@
             bytes_accessed=2 * (modes * points + rows * modes + steps * points),
             transcendentals=0,
         ),
-    )(pars, gains.reshape(1, steps), load_index.reshape(1, channels), loads, phi, shapes)
+    )(damping.reshape(1, owned), frequency.reshape(1, owned), gains, load_index.reshape(1, channels), loads, phi, shapes)
+    return hand_over(*results)
 
 
 def carried_in(value, axis, join, neutral):

time: 57.2 us -> 120 us (2.10)
  Pallas kernels: 48.9 us -> 120 us
  local copies, waits for them, and re-layouts: 6.04 us -> 0 us
  other arithmetic: 1.35 us -> 0 us
    pallas_call x0 -> x1, Pallas kernels: none -> 72.6 us  [hand_over(): pl.pallas_call(copies, out_shape=tuple((jax.ShapeDtypeStruct(a.shape, a.d...]
    unnamed x2 -> x0, local copies, waits for them, and re-layouts: 4.79 us -> none
    pallas_call x1, Pallas kernels: 48.9 us -> 46.9 us  [fused(): pl.pallas_call(functools.partial(kernel, tms), out_shape=(jax.ShapeDtypeS...]
    reshape x1 -> x0, local copies, waits for them, and re-layouts: 1.25 us -> none  [fused(): gains.reshape(1, steps)]
where the time goes in v2:
time: 120 us
  Pallas kernels  120 us (100%)
    pallas_call x1, Pallas kernels, hand_over(): pl.pallas_call(copies, out_shape=tuple((jax.ShapeDtypeStruct(a.shape, a.d...  72.6 us
    pallas_call x1, Pallas kernels, fused(): pl.pallas_call(functools.partial(kernel, tms), out_shape=(jax.ShapeDtypeS...  46.9 us

profile of v2, /device:TPU:0, one launch (start us, length us, event | category | flops | bytes accessed | tf_op | source)
XLA Modules:
  0.0 120.1 jit_solution(8775096442499066359)
XLA Ops:
  0.6 46.9 %shard_map.86 = (bf16[384,2048]{1,0:T(8,128)(2,1)}, f32[512,384]{1,0:T(8,128)}) custom-call(f32[1,512]{1,0:T(1,128)} %bitcast.3, f32[1,512]{1,0:T(1,128)} %bitcast.4, f32[384]{0:T(512)} %gains.1, s32[1,512]{1,0:T(1,128)} %bitcast.5, bf16[384,512]{1,0:T(8,128)(2,1)} %loads_in.1, bf16[768,4096]{1,0:T(8,128)(2,1)} %phi.1, bf16[4096,2048]{1,0:T(8,128)(2,1)} %shapes.1), custom_call_target="tpu_custom_call" | custom-call | flops 11274289152 | bytes 24641536 | tf_op jit(solution)/shard_map/pallas_call | solution.py:453
  47.5 72.6 %shard_map.87 = (bf16[384,2048]{1,0:T(8,128)(2,1)}, f32[512,384]{1,0:T(8,128)}) custom-call(bf16[384,2048]{1,0:T(8,128)(2,1)} %get-tuple-element.4.refs_0_, f32[512,384]{1,0:T(8,128)} %get-tuple-element.5.refs_1_), custom_call_target="tpu_custom_call" | custom-call | bytes 4718592 | tf_op jit(solution)/shard_map/pallas_call | solution.py:433

commit v3 on v2

--- a/solution.py
+++ b/solution.py
@@ -31,7 +31,7 @@
 
 def kernel(
     tms, damping, frequency, gains, index, loads_in, phi, shapes, field, hist,
-    pars, onehot, spread, loads, phi_buf, shapes_buf, tx_core, rx_core, own, tx_d, tx_x, tx_y, rx_d, rx_x, rx_y,
+    pars, onehot, spread, loads, row_loads, phi_buf, shapes_buf, tx_core, rx_core, own, tx_d, tx_x, tx_y, rx_d, rx_x, rx_y,
     mod, tx_tm, rx_tm, carry, gath, acc, turned, rounded,
     send, recv, loads_sem, phi_sem, shapes_sem, turned_sem, field_sem,
 ):
@@ -164,11 +164,11 @@
         place = lax.broadcasted_iota(jnp.int32, (channels, 128), 1) + j * 128
         onehot[:, j * 128:(j + 1) * 128] = jnp.where(place == names, 1.0, 0.0).astype(jnp.bfloat16)
     loads_copy.wait()
+    row_loads[...] = jnp.dot(loads[...], onehot[...], preferred_element_type=jnp.float32).astype(jnp.bfloat16)
 
     def partial_modal(q, r, s):
         phi_copy(q, r, s).wait()
-        chosen = jnp.dot(onehot[...], phi_buf[s, q, r], preferred_element_type=jnp.float32)
-        return jnp.dot(loads[...], chosen.astype(jnp.bfloat16), preferred_element_type=jnp.float32)
+        return jnp.dot(row_loads[...], phi_buf[s, q, r], preferred_element_type=jnp.float32)
 
     def for_partner(q, s):
         tx_core[q, s] = partial_modal(q, 1, s).astype(jnp.bfloat16)
@@ -416,26 +416,33 @@
 
     def copies(*refs):
         count = len(arrays)
-        started = []
+        sources, targets, held, (into, out) = refs[:count], refs[count:2 * count], refs[2 * count:3 * count], refs[3 * count:]
+        pairs = []
         for n in range(count):
             rows = arrays[n].shape[0] // pieces
             for piece in range(pieces):
                 at = pl.ds(piece * rows, rows)
-                started.append(
-                    pltpu.make_async_copy(refs[n].at[at], refs[count + n].at[at], refs[2 * count].at[n, piece])
-                )
-        for copy in started:
-            copy.start()
-        for copy in started:
-            copy.wait()
-
-    large = pl.BlockSpec(memory_space=pltpu.HBM)
+                pairs.append((
+                    pltpu.make_async_copy(sources[n].at[at], held[n].at[at], into.at[n, piece]),
+                    pltpu.make_async_copy(held[n].at[at], targets[n].at[at], out.at[n, piece]),
+                ))
+        for first, _ in pairs:
+            first.start()
+        for first, second in pairs:
+            first.wait()
+            second.start()
+        for _, second in pairs:
+            second.wait()
+
+    place = pl.BlockSpec(memory_space=pltpu.HBM)
     return pl.pallas_call(
         copies,
         out_shape=tuple(jax.ShapeDtypeStruct(a.shape, a.dtype) for a in arrays),
-        in_specs=[large] * len(arrays),
-        out_specs=(large,) * len(arrays),
-        scratch_shapes=[pltpu.SemaphoreType.DMA((len(arrays), pieces))],
+        in_specs=[place] * len(arrays),
+        out_specs=(place,) * len(arrays),
+        scratch_shapes=[pltpu.VMEM(a.shape, a.dtype) for a in arrays]
+        + [pltpu.SemaphoreType.DMA((len(arrays), pieces))] * 2,
+        compiler_params=pltpu.CompilerParams(vmem_limit_bytes=16 * 1024 * 1024),
         cost_estimate=pl.CostEstimate(
             flops=0, bytes_accessed=sum(2 * a.size * a.dtype.itemsize for a in arrays), transcendentals=0
         ),
@@ -463,6 +470,7 @@
             pltpu.VMEM((channels, rows), b16),
             pltpu.VMEM((steps, 128), f32),
             pltpu.VMEM((steps, channels), b16),
+            pltpu.VMEM((steps, rows), b16),
             pltpu.VMEM((NSUB, 4, 2, rows, width), b16),
             pltpu.VMEM((modes, points), b16),
             pltpu.VMEM((4, NSUB, steps, width), b16),
@@ -489,7 +497,7 @@
             collective_id=0, has_side_effects=True, vmem_limit_bytes=56 * 1024 * 1024
         ),
         cost_estimate=pl.CostEstimate(
-            flops=2 * steps * modes * (points + channels) + 2 * channels * rows * modes,
+            flops=2 * steps * (modes * (points + rows) + channels * rows),
             bytes_accessed=2 * (modes * points + rows * modes + steps * points),
             transcendentals=0,
         ),

time: 120 us -> 51.3 us (0.43)
  Pallas kernels: 120 us -> 47.9 us
  local copies, waits for them, and re-layouts: 0 us -> 2.53 us
    pallas_call x1, Pallas kernels: 72.6 us -> 3.28 us  [hand_over(): pl.pallas_call(copies, out_shape=tuple((jax.ShapeDtypeStruct(a.shape, a.d...]
    unnamed x0 -> x4, local copies, waits for them, and re-layouts: none -> 2.53 us
    pallas_call x1, Pallas kernels: 46.9 us -> 44.7 us  [fused(): pl.pallas_call(functools.partial(kernel, tms), out_shape=(jax.ShapeDtypeS...]
where the time goes in v3:
time: 51.3 us; the launch traced here: 51.1 us
  Pallas kernels  47.9 us (93%)
  local copies, waits for them, and re-layouts  2.53 us (5%)
  between operations  0.65 us (1%)
    pallas_call x1, Pallas kernels, fused(): pl.pallas_call(functools.partial(kernel, tms), out_shape=(jax.ShapeDtypeS...  44.7 us
    pallas_call x1, Pallas kernels, hand_over(): pl.pallas_call(copies, out_shape=tuple((jax.ShapeDtypeStruct(a.shape, a.d...  3.28 us
    unnamed x4, local copies, waits for them, and re-layouts  2.53 us

profile of v3, /device:TPU:0, one launch (start us, length us, event | category | flops | bytes accessed | tf_op | source)
XLA Modules:
  0.0 51.1 jit_solution(12165682394459855274)
XLA Ops:
  0.6 44.7 %shard_map.86 = (bf16[384,2048]{1,0:T(8,128)(2,1)}, f32[512,384]{1,0:T(8,128)}) custom-call(f32[1,512]{1,0:T(1,128)} %bitcast.3, f32[1,512]{1,0:T(1,128)} %bitcast.4, f32[384]{0:T(512)} %gains.1, s32[1,512]{1,0:T(1,128)} %bitcast.5, bf16[384,512]{1,0:T(8,128)(2,1)} %loads_in.1, bf16[768,4096]{1,0:T(8,128)(2,1)} %phi.1, bf16[4096,2048]{1,0:T(8,128)(2,1)} %shapes.1), custom_call_target="tpu_custom_call" | custom-call | flops 9160359936 | bytes 24641536 | tf_op jit(solution)/shard_map/pallas_call | solution.py:460
  45.3 0.0 copy-start
  45.3 1.4 %copy-done = bf16[384,2048]{1,0:T(8,128)(2,1)S(1)} copy-done((bf16[384,2048]{1,0:T(8,128)(2,1)S(1)}, bf16[384,2048]{1,0:T(8,128)(2,1)}, u32[]{:S(2)}) %copy-start) | copy-done | bytes 1572888
  46.7 0.0 copy-start.1
  46.7 1.1 %copy-done.1 = f32[512,384]{1,0:T(8,128)S(1)} copy-done((f32[512,384]{1,0:T(8,128)S(1)}, f32[512,384]{1,0:T(8,128)}, u32[]{:S(2)}) %copy-start.1) | copy-done | bytes 786456
  47.8 3.3 %shard_map.87 = (bf16[384,2048]{1,0:T(8,128)(2,1)}, f32[512,384]{1,0:T(8,128)}) custom-call(bf16[384,2048]{1,0:T(8,128)(2,1)S(1)} %copy-done, f32[512,384]{1,0:T(8,128)S(1)} %copy-done.1), custom_call_target="tpu_custom_call" | custom-call | bytes 4718592 | tf_op jit(solution)/shard_map/pallas_call | solution.py:438
Async XLA Ops:
  45.3 1.4 %copy-start = (bf16[384,2048]{1,0:T(8,128)(2,1)S(1)}, bf16[384,2048]{1,0:T(8,128)(2,1)}, u32[]{:S(2)}) copy-start(bf16[384,2048]{1,0:T(8,128)(2,1)} %get-tuple-element.4.refs_0_) | copy-start | bytes 4718596
  46.7 1.1 %copy-start.1 = (f32[512,384]{1,0:T(8,128)S(1)}, f32[512,384]{1,0:T(8,128)}, u32[]{:S(2)}) copy-start(f32[512,384]{1,0:T(8,128)} %get-tuple-element.5.refs_1_) | copy-start | bytes 2359300

commit v4 on v2

--- a/solution.py
+++ b/solution.py
@@ -9,6 +9,7 @@
 
 MESH = pl.DeviceIdType.MESH
 NSUB = 2
+BLOCKS = ((0, 0), (0, 1), (1, 0), (2, 0), (1, 1), (2, 1), (3, 0), (3, 1))
 SEGS = 8
 CORE, DA, DB, XA, XB, YA, YB = 0, 4, 5, 6, 7, 8, 9
 GXA, GXB, GYA, GYB, GP, FA, FB, PX, PY, PD, TM = 10, 11, 12, 13, 14, 15, 16, 17, 18, 19, 20
@@ -30,10 +31,10 @@
 
 
 def kernel(
-    tms, damping, frequency, gains, index, loads_in, phi, shapes, field, hist,
-    pars, onehot, spread, loads, phi_buf, shapes_buf, tx_core, rx_core, own, tx_d, tx_x, tx_y, rx_d, rx_x, rx_y,
-    mod, tx_tm, rx_tm, carry, gath, acc, turned, rounded,
-    send, recv, loads_sem, phi_sem, shapes_sem, turned_sem, field_sem,
+    tms, damping, frequency, gains, index, loads, phi, shapes, field, hist,
+    pars, onehot, spread, row_loads, phi_buf, shapes_buf, tx_core, rx_core, own, tx_d, tx_x, tx_y, rx_d, rx_x, rx_y,
+    mod, tx_tm, rx_tm, carry, gath, acc,
+    send, recv, phi_sem, shapes_sem,
 ):
     steps = loads.shape[0]
     half = steps // 2
@@ -94,7 +95,7 @@
         return piece(tx_y, rx_y, low, YB, s, yn)
 
     def lanes_of(q, r, s):
-        return pl.ds(((s * 4 + q) * 2 + r) * width, width)
+        return pl.ds((s * 8 + BLOCKS.index((q, r))) * width, width)
 
     def gathered(src, dst, span, kind, s, to):
         return remote(gath.at[span, lanes_of(*src, s)], gath.at[span, lanes_of(*dst, s)], kind, s, to)
@@ -144,7 +145,6 @@
             shapes.at[pl.ds(start, width), :], shapes_buf.at[lanes_of(q, r, s), :], shapes_sem.at[s, q, r]
         )
 
-    loads_copy = pltpu.make_async_copy(loads_in, loads, loads_sem)
     order = (3, 1, 2, 0)
 
     barrier = pltpu.get_barrier_semaphore()
@@ -153,26 +153,27 @@
     for dk in range(1, tms):
         to = lax.rem(me + dk, tms)
         pl.semaphore_signal(barrier, inc=1, device_id={"tm": to}, device_id_type=MESH)
-    loads_copy.start()
-    for s in range(NSUB):
+    def start_phi(s):
         for q in order:
             phi_copy(q, 1, s).start()
             phi_copy(q, 0, s).start()
+
+    start_phi(0)
 
     names = jnp.broadcast_to(index[...] - d * rows, (128, channels)).T
     for j in range(rows // 128):
         place = lax.broadcasted_iota(jnp.int32, (channels, 128), 1) + j * 128
         onehot[:, j * 128:(j + 1) * 128] = jnp.where(place == names, 1.0, 0.0).astype(jnp.bfloat16)
-    loads_copy.wait()
+    row_loads[...] = jnp.dot(loads[...], onehot[...], preferred_element_type=jnp.float32).astype(jnp.bfloat16)
 
     def partial_modal(q, r, s):
         phi_copy(q, r, s).wait()
-        chosen = jnp.dot(onehot[...], phi_buf[s, q, r], preferred_element_type=jnp.float32)
-        return jnp.dot(loads[...], chosen.astype(jnp.bfloat16), preferred_element_type=jnp.float32)
+        return jnp.dot(row_loads[...], phi_buf[s, q, r], preferred_element_type=jnp.float32)
 
     def for_partner(q, s):
         tx_core[q, s] = partial_modal(q, 1, s).astype(jnp.bfloat16)
         if q == order[0] and s == 0:
+            start_phi(1)
             pl.semaphore_wait(barrier, 3 + tms - 1)
         core_copy(q, s).start()
 
@@ -312,12 +313,7 @@
         for copy in (gxa(s), gyb(s), gp(s), gxb(s), gya(s)):
             copy.start()
         for j in range(cols):
-            turned[s * width + j * 128:s * width + (j + 1) * 128, :] = mod[s, j].T
-        turned_copy(s).start()
-
-    def turned_copy(s):
-        at = pl.ds(s * width, width)
-        return pltpu.make_async_copy(turned.at[at], hist.at[at], turned_sem.at[s])
+            hist[s * width + j * 128:s * width + (j + 1) * 128, :] = mod[s, j].T
 
     def forward(s):
         gxa(s).wait_recv()
@@ -336,16 +332,10 @@
         fb(s).wait_recv()
         pq(3, s).start()
 
-    def field_copy(n):
-        at = pl.ds(pl.multiple_of(n * tile, tile), tile)
-        return pltpu.make_async_copy(rounded.at[:, at], field.at[:, at], field_sem.at[n])
-
     def expand(first, count, mode):
         for block in range(first, first + count):
-            s, q = block // 4, block % 4
-            shapes_copy(q, 0, s).wait()
-            shapes_copy(q, 1, s).wait()
-        deep = pl.ds(first * 2 * width, count * 2 * width)
+            shapes_copy(*BLOCKS[block % 8], block // 8).wait()
+        deep = pl.ds(first * width, count * width)
 
         def one(n, _):
             at = pl.ds(pl.multiple_of(n * tile, tile), tile)
@@ -353,8 +343,7 @@
             if mode != "first":
                 value += acc[:, at]
             if mode == "last":
-                rounded[:, at] = value.astype(jnp.bfloat16)
-                field_copy(n).start()
+                field[:, at] = value.astype(jnp.bfloat16)
             else:
                 acc[:, at] = value
             return 0
@@ -363,9 +352,8 @@
 
     partials(0)
     for s in range(NSUB):
-        for q in range(4):
-            shapes_copy(q, 0, s).start()
-            shapes_copy(q, 1, s).start()
+        for q, r in BLOCKS:
+            shapes_copy(q, r, s).start()
     parameters()
     partials(1, lambda: pass_on(0))
     kept_0 = local_states(0)
@@ -373,30 +361,29 @@
     finish(0, kept_0)
     kept_1 = local_states(1)
     gp(0).wait_recv()
-    expand(0, 1, "first")
+    expand(0, 2, "first")
     forward(0)
     finish(1, kept_1)
     share(0)
+    expand(2, 2, "add")
     share_last(0)
     pq(1, 0).wait_recv()
     pq(2, 0).wait_recv()
-    expand(1, 2, "add")
+    expand(4, 2, "add")
     forward(1)
     pq(3, 0).wait_recv()
     gp(1).wait_recv()
-    expand(3, 2, "add")
+    expand(6, 4, "add")
     share(1)
-    share_last(1)
+    expand(10, 2, "add")
     pq(1, 1).wait_recv()
     pq(2, 1).wait_recv()
-    expand(5, 2, "add")
+    expand(12, 2, "add")
+    share_last(1)
+    expand(14, 1, "add")
     pq(3, 1).wait_recv()
-    expand(7, 1, "last")
-
-    for n in range(points // tile):
-        field_copy(n).wait()
-    for s in range(NSUB):
-        turned_copy(s).wait()
+    expand(15, 1, "last")
+
     for s in range(NSUB):
         for q in range(4):
             core_copy(q, s).wait_send()
@@ -429,13 +416,13 @@
         for copy in started:
             copy.wait()
 
-    large = pl.BlockSpec(memory_space=pltpu.HBM)
     return pl.pallas_call(
         copies,
         out_shape=tuple(jax.ShapeDtypeStruct(a.shape, a.dtype) for a in arrays),
-        in_specs=[large] * len(arrays),
-        out_specs=(large,) * len(arrays),
+        in_specs=[pl.BlockSpec(memory_space=pltpu.VMEM)] * len(arrays),
+        out_specs=(pl.BlockSpec(memory_space=pltpu.HBM),) * len(arrays),
         scratch_shapes=[pltpu.SemaphoreType.DMA((len(arrays), pieces))],
+        compiler_params=pltpu.CompilerParams(vmem_limit_bytes=16 * 1024 * 1024),
         cost_estimate=pl.CostEstimate(
             flops=0, bytes_accessed=sum(2 * a.size * a.dtype.itemsize for a in arrays), transcendentals=0
         ),
@@ -449,20 +436,20 @@
     b16, f32 = jnp.bfloat16, jnp.float32
     kinds = TM + tms - 1
     small = pl.BlockSpec(memory_space=pltpu.VMEM)
-    large = pl.BlockSpec(memory_space=pl.ANY)
+    large = pl.BlockSpec(memory_space=pltpu.HBM)
     results = pl.pallas_call(
         functools.partial(kernel, tms),
         out_shape=(
             jax.ShapeDtypeStruct((steps, points), b16),
             jax.ShapeDtypeStruct((owned, steps), f32),
         ),
-        in_specs=[small, small, small, small, large, large, large],
-        out_specs=(large, large),
+        in_specs=[small, small, small, small, small, large, large],
+        out_specs=(small, small),
         scratch_shapes=[
             pltpu.VMEM((8, owned), f32),
             pltpu.VMEM((channels, rows), b16),
             pltpu.VMEM((steps, 128), f32),
-            pltpu.VMEM((steps, channels), b16),
+            pltpu.VMEM((steps, rows), b16),
             pltpu.VMEM((NSUB, 4, 2, rows, width), b16),
             pltpu.VMEM((modes, points), b16),
             pltpu.VMEM((4, NSUB, steps, width), b16),
@@ -475,21 +462,16 @@
             pltpu.VMEM((NSUB, 8, width), f32),
             pltpu.VMEM((steps, modes), b16),
             pltpu.VMEM((steps, points), f32),
-            pltpu.VMEM((owned, steps), f32),
-            pltpu.VMEM((steps, points), b16),
             pltpu.SemaphoreType.DMA((NSUB, kinds)),
             pltpu.SemaphoreType.DMA((NSUB, kinds)),
-            pltpu.SemaphoreType.DMA,
             pltpu.SemaphoreType.DMA((NSUB, 4, 2)),
             pltpu.SemaphoreType.DMA((NSUB, 4, 2)),
-            pltpu.SemaphoreType.DMA((NSUB,)),
-            pltpu.SemaphoreType.DMA((points // min(512, points),)),
         ],
         compiler_params=pltpu.CompilerParams(
-            collective_id=0, has_side_effects=True, vmem_limit_bytes=56 * 1024 * 1024
+            collective_id=0, has_side_effects=True, vmem_limit_bytes=50 * 1024 * 1024
         ),
         cost_estimate=pl.CostEstimate(
-            flops=2 * steps * modes * (points + channels) + 2 * channels * rows * modes,
+            flops=2 * steps * (modes * (points + rows) + channels * rows),
             bytes_accessed=2 * (modes * points + rows * modes + steps * points),
             transcendentals=0,
         ),

time: 120 us -> 48.3 us (0.40)
  Pallas kernels: 120 us -> 43.7 us
  local copies, waits for them, and re-layouts: 0 us -> 3.71 us
    pallas_call x1, Pallas kernels: 72.6 us -> 1.46 us  [hand_over(): pl.pallas_call(copies, out_shape=tuple((jax.ShapeDtypeStruct(a.shape, a.d...]
    pallas_call x1, Pallas kernels: 46.9 us -> 42.2 us  [fused(): pl.pallas_call(functools.partial(kernel, tms), out_shape=(jax.ShapeDtypeS...]
    unnamed x0 -> x10, local copies, waits for them, and re-layouts: none -> 3.71 us
where the time goes in v4:
time: 48.3 us; the launch traced here: 48.1 us
  Pallas kernels  43.7 us (90%)
  local copies, waits for them, and re-layouts  3.71 us (8%)
  between operations  0.65 us (1%)
    pallas_call x1, Pallas kernels, fused(): pl.pallas_call(functools.partial(kernel, tms), out_shape=(jax.ShapeDtypeS...  42.2 us
    unnamed x10, local copies, waits for them, and re-layouts  3.71 us
    pallas_call x1, Pallas kernels, hand_over(): pl.pallas_call(copies, out_shape=tuple((jax.ShapeDtypeStruct(a.shape, a.d...  1.46 us

profile of v4, /device:TPU:0, one launch (start us, length us, event | category | flops | bytes accessed | tf_op | source)
XLA Modules:
  0.0 48.1 jit_solution(2818604909363000586)
XLA Ops:
  0.6 0.0 copy-start
  0.6 1.0 %copy-done = bf16[384,512]{1,0:T(8,128)(2,1)S(1)} copy-done((bf16[384,512]{1,0:T(8,128)(2,1)S(1)}, bf16[384,512]{1,0:T(8,128)(2,1)}, u32[]{:S(2)}) %copy-start) | copy-done | bytes 393240
  1.6 0.0 copy-start.1
  1.6 0.7 %copy-done.1 = f32[512]{0:T(512)S(1)} copy-done((f32[512]{0:T(512)S(1)}, f32[512]{0:T(512)}, u32[]{:S(2)}) %copy-start.1) | copy-done | bytes 2072
  2.3 0.0 copy-start.2
  2.3 0.7 %copy-done.2 = f32[512]{0:T(512)S(1)} copy-done((f32[512]{0:T(512)S(1)}, f32[512]{0:T(512)}, u32[]{:S(2)}) %copy-start.2) | copy-done | bytes 2072
  3.0 0.0 copy-start.3
  3.0 0.7 %copy-done.3 = f32[384]{0:T(512)S(1)} copy-done((f32[384]{0:T(512)S(1)}, f32[384]{0:T(512)}, u32[]{:S(2)}) %copy-start.3) | copy-done | bytes 1560
  3.7 0.0 copy-start.4
  3.7 0.7 %copy-done.4 = s32[512]{0:T(512)S(1)} copy-done((s32[512]{0:T(512)S(1)}, s32[512]{0:T(512)}, u32[]{:S(2)}) %copy-start.4) | copy-done | bytes 2072
  4.4 42.2 %shard_map.86 = (bf16[384,2048]{1,0:T(8,128)(2,1)S(1)}, f32[512,384]{1,0:T(8,128)S(1)}) custom-call(f32[1,512]{1,0:T(1,128)S(1)} %bitcast.3, f32[1,512]{1,0:T(1,128)S(1)} %bitcast.4, f32[384]{0:T(512)S(1)} %copy-done.3, s32[1,512]{1,0:T(1,128)S(1)} %bitcast.5, bf16[384,512]{1,0:T(8,128)(2,1)S(1)} %copy-done, bf16[768,4096]{1,0:T(8,128)(2,1)} %phi.1, ...), custom_call_target="tpu_custom_call" | custom-call | flops 9160359936 | bytes 24641536 | tf_op jit(solution)/shard_map/pallas_call | solution.py:440
  46.6 1.5 %shard_map.87 = (bf16[384,2048]{1,0:T(8,128)(2,1)}, f32[512,384]{1,0:T(8,128)}) custom-call(bf16[384,2048]{1,0:T(8,128)(2,1)S(1)} %get-tuple-element.4.refs_0_, f32[512,384]{1,0:T(8,128)S(1)} %get-tuple-element.5.refs_1_), custom_call_target="tpu_custom_call" | custom-call | bytes 4718592 | tf_op jit(solution)/shard_map/pallas_call | solution.py:419
Async XLA Ops:
  0.6 1.0 %copy-start = (bf16[384,512]{1,0:T(8,128)(2,1)S(1)}, bf16[384,512]{1,0:T(8,128)(2,1)}, u32[]{:S(2)}) copy-start(bf16[384,512]{1,0:T(8,128)(2,1)} %loads.1) | copy-start | bytes 1179652
  1.6 0.7 %copy-start.1 = (f32[512]{0:T(512)S(1)}, f32[512]{0:T(512)}, u32[]{:S(2)}) copy-start(f32[512]{0:T(512)} %param.10) | copy-start | bytes 6148
  2.3 0.7 %copy-start.2 = (f32[512]{0:T(512)S(1)}, f32[512]{0:T(512)}, u32[]{:S(2)}) copy-start(f32[512]{0:T(512)} %param.11) | copy-start | bytes 6148
  3.0 0.7 %copy-start.3 = (f32[384]{0:T(512)S(1)}, f32[384]{0:T(512)}, u32[]{:S(2)}) copy-start(f32[384]{0:T(512)} %gains.1) | copy-start | bytes 4612
  3.7 0.7 %copy-start.4 = (s32[512]{0:T(512)S(1)}, s32[512]{0:T(512)}, u32[]{:S(2)}) copy-start(s32[512]{0:T(512)} %param.9) | copy-start | bytes 6148

commit v5 on v4

--- a/solution.py
+++ b/solution.py
@@ -10,7 +10,7 @@
 MESH = pl.DeviceIdType.MESH
 NSUB = 2
 BLOCKS = ((0, 0), (0, 1), (1, 0), (2, 0), (1, 1), (2, 1), (3, 0), (3, 1))
-SEGS = 8
+SEGS = 16
 CORE, DA, DB, XA, XB, YA, YB = 0, 4, 5, 6, 7, 8, 9
 GXA, GXB, GYA, GYB, GP, FA, FB, PX, PY, PD, TM = 10, 11, 12, 13, 14, 15, 16, 17, 18, 19, 20
 
@@ -31,7 +31,7 @@
 
 
 def kernel(
-    tms, damping, frequency, gains, index, loads, phi, shapes, field, hist,
+    tms, packed, loads, phi, shapes, field, hist,
     pars, onehot, spread, row_loads, phi_buf, shapes_buf, tx_core, rx_core, own, tx_d, tx_x, tx_y, rx_d, rx_x, rx_y,
     mod, tx_tm, rx_tm, carry, gath, acc,
     send, recv, phi_sem, shapes_sem,
@@ -39,6 +39,10 @@
     steps = loads.shape[0]
     half = steps // 2
     owned = pars.shape[1]
+    damping = packed[pl.ds(0, owned)].reshape(1, owned)
+    frequency = packed[pl.ds(owned, owned)].reshape(1, owned)
+    index = packed[pl.ds(2 * owned, loads.shape[1])].reshape(1, loads.shape[1])
+    gains = packed[pl.ds(2 * owned + loads.shape[1], steps)].reshape(1, steps)
     width = owned // NSUB
     cols = width // 128
     seg = steps // SEGS
@@ -160,9 +164,9 @@
 
     start_phi(0)
 
-    names = jnp.broadcast_to(index[...] - d * rows, (128, channels)).T
+    names = jnp.broadcast_to(index - (d * rows).astype(jnp.float32), (128, channels)).T
     for j in range(rows // 128):
-        place = lax.broadcasted_iota(jnp.int32, (channels, 128), 1) + j * 128
+        place = (lax.broadcasted_iota(jnp.int32, (channels, 128), 1) + j * 128).astype(jnp.float32)
         onehot[:, j * 128:(j + 1) * 128] = jnp.where(place == names, 1.0, 0.0).astype(jnp.bfloat16)
     row_loads[...] = jnp.dot(loads[...], onehot[...], preferred_element_type=jnp.float32).astype(jnp.bfloat16)
 
@@ -203,16 +207,16 @@
             own[s, q] = partial_modal(q, 0, s)
 
     def parameters():
-        x = 2.0 * damping[...]
+        x = 2.0 * damping
         series = jnp.ones_like(x)
         for n in range(12, 1, -1):
             series = 1.0 - x * series / n
         drive = jnp.sqrt(jnp.where(x < 0.5, x * series, 1.0 - jnp.exp(-x)))
-        radius = jnp.exp(-damping[...])
-        pars[0:1, :] = radius * jnp.cos(frequency[...])
-        pars[1:2, :] = radius * jnp.sin(frequency[...])
+        radius = jnp.exp(-damping)
+        pars[0:1, :] = radius * jnp.cos(frequency)
+        pars[1:2, :] = radius * jnp.sin(frequency)
         pars[2:3, :] = drive
-        spread[...] = jnp.broadcast_to(gains[...].reshape(1, steps), (128, steps)).T
+        spread[...] = jnp.broadcast_to(gains, (128, steps)).T
 
     def pass_on(s):
         db(s).wait_recv()
@@ -235,9 +239,10 @@
             gain = spread[at, :]
             out = []
             for j in range(cols):
-                re, im = cmul(*coefs[j], *waves[j])
-                re = gain * re + mod[s, j, at, :]
-                im = gain * im
+                cr, ci = gain * coefs[j][0], gain * coefs[j][1]
+                wr, wi = waves[j]
+                re = (cr * wr + mod[s, j, at, :]) - ci * wi
+                im = cr * wi + ci * wr
                 if store:
                     mod[s, j, at, :] = re
                 out.append((re, im))
@@ -434,6 +439,7 @@
     rows, points, modes = phi.shape[0], shapes.shape[1], shapes.shape[0]
     width = owned // NSUB
     b16, f32 = jnp.bfloat16, jnp.float32
+    packed = jnp.concatenate([damping, frequency, load_index.astype(f32), gains])
     kinds = TM + tms - 1
     small = pl.BlockSpec(memory_space=pltpu.VMEM)
     large = pl.BlockSpec(memory_space=pltpu.HBM)
@@ -443,7 +449,7 @@
             jax.ShapeDtypeStruct((steps, points), b16),
             jax.ShapeDtypeStruct((owned, steps), f32),
         ),
-        in_specs=[small, small, small, small, small, large, large],
+        in_specs=[small, small, large, large],
         out_specs=(small, small),
         scratch_shapes=[
             pltpu.VMEM((8, owned), f32),
@@ -475,7 +481,7 @@
             bytes_accessed=2 * (modes * points + rows * modes + steps * points),
             transcendentals=0,
         ),
-    )(damping.reshape(1, owned), frequency.reshape(1, owned), gains, load_index.reshape(1, channels), loads, phi, shapes)
+    )(packed, loads, phi, shapes)
     return hand_over(*results)
 
 

time: 48.3 us -> 46.9 us (0.971)
  local copies, waits for them, and re-layouts: 3.71 us -> 1 us
  other arithmetic: 0 us -> 1.41 us
    unnamed x10 -> x2, local copies, waits for them, and re-layouts: 3.71 us -> 1 us
    concatenate x0 -> x1, other arithmetic: none -> 0.72 us  [fused(): jnp.concatenate([damping, frequency, load_index.astype(f32), gains])]
    convert_element_type x0 -> x1, other arithmetic: none -> 0.68 us  [fused(): load_index.astype(f32)]
where the time goes in v5:
time: 46.9 us; the launch traced here: 46.7 us
  Pallas kernels  43.6 us (93%)
  other arithmetic  1.41 us (3%)
  local copies, waits for them, and re-layouts  1 us (2%)
  between operations  0.64 us (1%)
    pallas_call x1, Pallas kernels, fused(): pl.pallas_call(functools.partial(kernel, tms), out_shape=(jax.ShapeDtypeS...  42.2 us
    pallas_call x1, Pallas kernels, hand_over(): pl.pallas_call(copies, out_shape=tuple((jax.ShapeDtypeStruct(a.shape, a.d...  1.46 us
    unnamed x2, local copies, waits for them, and re-layouts  1 us

profile of v5, /device:TPU:0, one launch (start us, length us, event | category | flops | bytes accessed | tf_op | source)
XLA Modules:
  0.0 46.7 jit_solution(7379659529368583802)
XLA Ops:
  0.6 0.7 %convert_element_type.3 = f32[512]{0:T(512)S(1)} convert(s32[512]{0:T(512)} %param.9) | non-fusion elementwise | flops 512 | bytes 4096 | tf_op jit(solution)/shard_map/convert_element_type | solution.py:442
  1.3 0.7 %pad_maximum_fusion.packed = f32[1920]{0:T(1024)S(1)} fusion(f32[384]{0:T(512)} %param.12, f32[512]{0:T(512)S(1)} %convert_element_type.3, f32[512]{0:T(512)} %param.11, f32[512]{0:T(512)} %param.10), kind=kLoop, calls=%fused_computation | loop fusion | flops 5760 | bytes 15360 | tf_op jit(solution)/shard_map/concatenate | solution.py:442
  2.0 0.0 copy-start
  2.0 1.0 %copy-done = bf16[384,512]{1,0:T(8,128)(2,1)S(1)} copy-done((bf16[384,512]{1,0:T(8,128)(2,1)S(1)}, bf16[384,512]{1,0:T(8,128)(2,1)}, u32[]{:S(2)}) %copy-start) | copy-done | bytes 393240
  3.0 42.2 %shard_map.86 = (bf16[384,2048]{1,0:T(8,128)(2,1)S(1)}, f32[512,384]{1,0:T(8,128)S(1)}) custom-call(f32[1920]{0:T(1024)S(1)} %pad_maximum_fusion.packed, bf16[384,512]{1,0:T(8,128)(2,1)S(1)} %copy-done, bf16[768,4096]{1,0:T(8,128)(2,1)} %phi.1, bf16[4096,2048]{1,0:T(8,128)(2,1)} %shapes.1), custom_call_target="tpu_custom_call" | custom-call | flops 9160359936 | bytes 24641536 | tf_op jit(solution)/shard_map/pallas_call | solution.py:446
  45.2 1.5 %shard_map.87 = (bf16[384,2048]{1,0:T(8,128)(2,1)}, f32[512,384]{1,0:T(8,128)}) custom-call(bf16[384,2048]{1,0:T(8,128)(2,1)S(1)} %get-tuple-element.4.refs_0_, f32[512,384]{1,0:T(8,128)S(1)} %get-tuple-element.5.refs_1_), custom_call_target="tpu_custom_call" | custom-call | bytes 4718592 | tf_op jit(solution)/shard_map/pallas_call | solution.py:424
Async XLA Ops:
  2.0 1.0 %copy-start = (bf16[384,512]{1,0:T(8,128)(2,1)S(1)}, bf16[384,512]{1,0:T(8,128)(2,1)}, u32[]{:S(2)}) copy-start(bf16[384,512]{1,0:T(8,128)(2,1)} %loads.1) | copy-start | bytes 1179652

commit v6 on v5

--- a/solution.py
+++ b/solution.py
@@ -8,7 +8,7 @@
 from jax.sharding import PartitionSpec as P
 
 MESH = pl.DeviceIdType.MESH
-NSUB = 2
+NSUB = 4
 BLOCKS = ((0, 0), (0, 1), (1, 0), (2, 0), (1, 1), (2, 1), (3, 0), (3, 1))
 SEGS = 16
 CORE, DA, DB, XA, XB, YA, YB = 0, 4, 5, 6, 7, 8, 9
@@ -177,7 +177,8 @@
     def for_partner(q, s):
         tx_core[q, s] = partial_modal(q, 1, s).astype(jnp.bfloat16)
         if q == order[0] and s == 0:
-            start_phi(1)
+            for part in range(1, NSUB):
+                start_phi(part)
             pl.semaphore_wait(barrier, 3 + tms - 1)
         core_copy(q, s).start()
 
@@ -355,39 +356,62 @@
 
         lax.fori_loop(0, points // tile, one, 0)
 
+    def sides(s):
+        pq(1, s).wait_recv()
+        pq(2, s).wait_recv()
+
+    def corner(s):
+        pq(3, s).wait_recv()
+        gp(s + 1).wait_recv()
+
     partials(0)
     for s in range(NSUB):
         for q, r in BLOCKS:
             shapes_copy(q, r, s).start()
     parameters()
     partials(1, lambda: pass_on(0))
+    partials(2, lambda: pass_on(1))
     kept_0 = local_states(0)
-    pass_on(1)
+    partials(3, lambda: pass_on(2))
     finish(0, kept_0)
     kept_1 = local_states(1)
+    pass_on(3)
+    forward(0)
+    finish(1, kept_1)
+    kept_2 = local_states(2)
+    share(0)
     gp(0).wait_recv()
     expand(0, 2, "first")
-    forward(0)
-    finish(1, kept_1)
-    share(0)
-    expand(2, 2, "add")
+    forward(1)
+    finish(2, kept_2)
+    kept_3 = local_states(3)
     share_last(0)
-    pq(1, 0).wait_recv()
-    pq(2, 0).wait_recv()
-    expand(4, 2, "add")
-    forward(1)
-    pq(3, 0).wait_recv()
-    gp(1).wait_recv()
+    sides(0)
+    expand(2, 4, "add")
+    share(1)
+    forward(2)
+    finish(3, kept_3)
+    share_last(1)
+    corner(0)
     expand(6, 4, "add")
-    share(1)
-    expand(10, 2, "add")
-    pq(1, 1).wait_recv()
-    pq(2, 1).wait_recv()
-    expand(12, 2, "add")
-    share_last(1)
-    expand(14, 1, "add")
-    pq(3, 1).wait_recv()
-    expand(15, 1, "last")
+    sides(1)
+    expand(10, 4, "add")
+    share(2)
+    forward(3)
+    share_last(2)
+    corner(1)
+    expand(14, 4, "add")
+    sides(2)
+    expand(18, 4, "add")
+    share(3)
+    corner(2)
+    expand(22, 4, "add")
+    sides(3)
+    expand(26, 4, "add")
+    share_last(3)
+    expand(30, 1, "add")
+    pq(3, 3).wait_recv()
+    expand(31, 1, "last")
 
     for s in range(NSUB):
         for q in range(4):

time: 46.9 us -> 53.2 us (1.13)
  Pallas kernels: 43.6 us -> 49.8 us
    pallas_call x1, Pallas kernels: 42.2 us -> 48.3 us  [fused(): pl.pallas_call(functools.partial(kernel, tms), out_shape=(jax.ShapeDtypeS...]
where the time goes in v6:
time: 53.2 us; the launch traced here: 53 us
  Pallas kernels  49.8 us (94%)
  other arithmetic  1.41 us (3%)
  local copies, waits for them, and re-layouts  1 us (2%)
  between operations  0.8 us (2%)
    pallas_call x1, Pallas kernels, fused(): pl.pallas_call(functools.partial(kernel, tms), out_shape=(jax.ShapeDtypeS...  48.3 us
    pallas_call x1, Pallas kernels, hand_over(): pl.pallas_call(copies, out_shape=tuple((jax.ShapeDtypeStruct(a.shape, a.d...  1.46 us

profile of v6, /device:TPU:0, one launch (start us, length us, event | category | flops | bytes accessed | tf_op | source)
XLA Modules:
  0.0 53.0 jit_solution(8294172018937193261)
XLA Ops:
  0.6 0.7 %convert_element_type.3 = f32[512]{0:T(512)S(1)} convert(s32[512]{0:T(512)} %param.9) | non-fusion elementwise | flops 512 | bytes 4096 | tf_op jit(solution)/shard_map/convert_element_type | solution.py:466
  1.3 0.7 %pad_maximum_fusion.packed = f32[1920]{0:T(1024)S(1)} fusion(f32[384]{0:T(512)} %param.12, f32[512]{0:T(512)S(1)} %convert_element_type.3, f32[512]{0:T(512)} %param.11, f32[512]{0:T(512)} %param.10), kind=kLoop, calls=%fused_computation | loop fusion | flops 5760 | bytes 15360 | tf_op jit(solution)/shard_map/concatenate | solution.py:466
  2.0 0.0 copy-start
  2.0 1.0 %copy-done = bf16[384,512]{1,0:T(8,128)(2,1)S(1)} copy-done((bf16[384,512]{1,0:T(8,128)(2,1)S(1)}, bf16[384,512]{1,0:T(8,128)(2,1)}, u32[]{:S(2)}) %copy-start) | copy-done | bytes 393240
  3.0 48.3 %shard_map.86 = (bf16[384,2048]{1,0:T(8,128)(2,1)S(1)}, f32[512,384]{1,0:T(8,128)S(1)}) custom-call(f32[1920]{0:T(1024)S(1)} %pad_maximum_fusion.packed, bf16[384,512]{1,0:T(8,128)(2,1)S(1)} %copy-done, bf16[768,4096]{1,0:T(8,128)(2,1)} %phi.1, bf16[4096,2048]{1,0:T(8,128)(2,1)} %shapes.1), custom_call_target="tpu_custom_call" | custom-call | flops 9160359936 | bytes 24641536 | tf_op jit(solution)/shard_map/pallas_call | solution.py:470
  51.3 1.5 %shard_map.87 = (bf16[384,2048]{1,0:T(8,128)(2,1)}, f32[512,384]{1,0:T(8,128)}) custom-call(bf16[384,2048]{1,0:T(8,128)(2,1)S(1)} %get-tuple-element.4.refs_0_, f32[512,384]{1,0:T(8,128)S(1)} %get-tuple-element.5.refs_1_), custom_call_target="tpu_custom_call" | custom-call | bytes 4718592 | tf_op jit(solution)/shard_map/pallas_call | solution.py:448
Async XLA Ops:
  2.0 1.0 %copy-start = (bf16[384,512]{1,0:T(8,128)(2,1)S(1)}, bf16[384,512]{1,0:T(8,128)(2,1)}, u32[]{:S(2)}) copy-start(bf16[384,512]{1,0:T(8,128)(2,1)} %loads.1) | copy-start | bytes 1179652
